TPU v7x, 32 devices: a whole 2x2x4 slice. The times are simulated.
32 devices in a mesh: lat: 4 (over y, x), lon: 8 (over z, core).
Axes of the slice: x: 2, y: 2, z: 4, core: 2. Of those that a mesh axis runs over, the one named last changes fastest.
Arguments:
- innovations: float32 [4096, 512], P(('lat', 'lon'))
- block_owner: int32 [4096, 1], P(('lat', 'lon')), may hold values from 0 to 31; in each aligned block of 128 rows (0 to 127, 128 to 255, ...) at most 8 rows name the same one
- block_lat: int32 [4096], P(('lat', 'lon')), may hold values from 0 to 124
- block_lon: int32 [4096], P(('lat', 'lon')), may hold values from 0 to 36
- block_count: int32 [32], P(('lat', 'lon')), may hold values from 1 to 128, 3584 in all
- error_weight: float32 [32, 512, 512], P(('lat', 'lon')), as said below
- courant_lon: float32 [32, 320, 512], P(None, 'lon', 'lat'), may hold values from -0.35 to 0.35
- courant_lat: float32 [32, 320, 512], P(None, 'lon', 'lat'), may hold values from -0.35 to 0.35
- background_std: float32 [32, 320, 512], P(None, 'lon', 'lat'), may hold values from 0.5 to 2
Outputs:
- solution: float32 [4096, 512], P(('lat', 'lon'))
- increment: float32 [32, 320, 512], P(None, 'lon', 'lat')
Inputs may be any that keep to these rules, and one draw needn't show every extreme that they name: `block_owner`: tile index is the lat index times the number of lon devices plus the lon index. Among the 128 block slots of one device no tile is named more than 8 times, and in every draw some device names some tile exactly 8 times. Only the first block_count slots of a device hold live blocks; some device holds 128 live blocks. `block_lat`: the footprint of 4 x 4 cells lies inside the tile. `block_lon`: the footprint of 4 x 4 cells lies inside the tile. `error_weight`: one matrix for the blocks of each device.
All inputs are finite; a program needn't handle non-finite values.
Results may differ from a plain program's by a relative error of at most 0.0003.
Values sent between devices are 32-bit elements; how exact they have to be, the bound alone decides.
A program may use at most 192 MiB of HBM per device.

v0:
```python
import jax
import jax.numpy as jnp
from jax import lax
from jax.sharding import PartitionSpec as P

LEV = 32
FOOT = 4
STEPS = 4
ITERS = 2


DIFFUSION = 0.15
PRECISE = lax.Precision.HIGHEST


def with_halo(array, sides, width, wrap):
    for axis, dim in sides:
        count, length = (lax.axis_size(axis), array.shape[dim])
        up = [(i, (i + 1) % count) for i in range(count if wrap else count - 1)]
        down = [(j, i) for i, j in up]
        last = lax.slice_in_dim(array, length - width, length, axis=dim)
        leading = lax.slice_in_dim(array, 0, width, axis=dim)
        before = lax.ppermute(last, axis, up)
        after = lax.ppermute(leading, axis, down)
        array = jnp.concatenate([before, array, after], axis=dim)
    return array


def extend(values, halo_width):
    flattened = values.reshape((-1,) + values.shape[-2:])
    flattened = with_halo(flattened, (("lon", 1),), halo_width, True)
    flattened = with_halo(flattened, (("lat", 2),), halo_width, False)
    return flattened.reshape(values.shape[:-2] + flattened.shape[-2:])


def stencil(padded, stencil_weights, halo_width):
    margin_cut = STEPS - halo_width + 1
    local_weights = stencil_weights[
        :,
        :,
        margin_cut : stencil_weights.shape[2] - margin_cut,
        margin_cut : stencil_weights.shape[3] - margin_cut,
    ]
    return (
        local_weights[0] * padded[:, 1:-1, 1:-1]
        + local_weights[1] * padded[:, 2:, 1:-1]
        + local_weights[2] * padded[:, :-2, 1:-1]
        + local_weights[3] * padded[:, 1:-1, 2:]
        + local_weights[4] * padded[:, 1:-1, :-2]
    )


def propagate(field_now, stencil_weights):
    for step_index in range(STEPS):
        field_now = stencil(extend(field_now, 1), stencil_weights, 1)
    return field_now


def trade_blocks(slot_rows, slot_depth):
    lat_count = lax.axis_size("lat")
    lon_count = lax.axis_size("lon")
    row_width = slot_rows.shape[-1]
    direct = slot_rows.reshape(lat_count * lon_count, slot_depth, row_width)
    arrived = lax.all_to_all(direct, ("lat", "lon"), split_axis=0, concat_axis=0, tiled=True)
    return arrived.reshape(lat_count * lon_count * slot_depth, row_width)


def pack_rows(block_rows, target, total_slots):
    holder = jnp.zeros((total_slots + 1, block_rows.shape[1]), block_rows.dtype)
    return holder.at[target].set(block_rows)[:total_slots]


def unpack_rows(slot_rows, target):
    padded = jnp.concatenate([slot_rows, jnp.zeros_like(slot_rows[:1])], axis=0)
    return padded[target]


def sample_field(field_now, cell_index, slot_total):
    picked = field_now.reshape(field_now.shape[0], -1)[:, cell_index]
    picked = picked.reshape(field_now.shape[0], slot_total, FOOT * FOOT)
    return picked.transpose(1, 0, 2).reshape(slot_total, -1)


def spread_rows(slot_rows, cell_index, field_shape):
    patches = (
        slot_rows.reshape(slot_rows.shape[0], LEV, FOOT * FOOT).transpose(1, 0, 2).reshape(LEV, -1)
    )
    flat_field = (
        jnp.zeros((LEV, field_shape[1] * field_shape[2]), jnp.float32)
        .at[:, cell_index]
        .add(patches)
    )
    return flat_field.reshape(field_shape)


def squares(residual):
    return lax.psum(jnp.sum(residual * residual), ("lat", "lon"))


def body(
    innovations,
    block_owner,
    block_lat,
    block_lon,
    block_count,
    error_weight,
    courant_lon,
    courant_lat,
    background_std,
):
    matrix = error_weight[0]
    block_total = innovations.shape[0]
    device_total = lax.axis_size("lat") * lax.axis_size("lon")
    slot_depth = 2 * block_total // device_total
    total_slots = device_total * slot_depth
    field_shape = courant_lon.shape
    is_live = jnp.arange(block_total) < block_count[0]
    owners = block_owner[:, 0]
    onehot = ((owners[:, None] == jnp.arange(device_total)[None, :]) & is_live[:, None]).astype(
        jnp.int32
    )
    before = jnp.sum((jnp.cumsum(onehot, axis=0) - onehot) * onehot, axis=1)
    target = jnp.where(is_live, owners * slot_depth + before, total_slots)
    anchor_rows = jnp.stack([block_lon, block_lat], axis=1)
    anchor_slots = pack_rows(anchor_rows, target, total_slots).reshape(device_total, slot_depth, 2)
    anchors = lax.all_to_all(
        anchor_slots, ("lat", "lon"), split_axis=0, concat_axis=0, tiled=True
    ).reshape(total_slots, 2)
    offsets = jnp.arange(FOOT, dtype=jnp.int32)
    cell_index = (
        (anchors[:, 0][:, None, None] + offsets[None, :, None]) * field_shape[2]
        + anchors[:, 1][:, None, None]
        + offsets[None, None, :]
    ).reshape(-1)
    centre = jnp.zeros_like(courant_lon) + (1.0 - 4.0 * DIFFUSION)
    raw_weights = jnp.stack(
        [
            centre,
            DIFFUSION - 0.5 * courant_lon,
            DIFFUSION + 0.5 * courant_lon,
            DIFFUSION - 0.5 * courant_lat,
            DIFFUSION + 0.5 * courant_lat,
        ]
    )
    wide_weights = extend(raw_weights, STEPS + 1)
    forward_weights = wide_weights[:, :, 1:-1, 1:-1]
    lat_first = lax.axis_index("lat") * field_shape[2] - STEPS
    lat_global = lat_first + jnp.arange(field_shape[2] + 2 * STEPS)
    inside = ((lat_global >= 0) & (lat_global < field_shape[2] * lax.axis_size("lat"))).astype(
        jnp.float32
    )
    adjoint_weights = (
        jnp.stack(
            [
                wide_weights[0, :, 1:-1, 1:-1],
                wide_weights[2, :, 2:, 1:-1],
                wide_weights[1, :, :-2, 1:-1],
                wide_weights[4, :, 1:-1, 2:],
                wide_weights[3, :, 1:-1, :-2],
            ]
        )
        * inside
    )
    variance = background_std * background_std

    def adjoint_spread(dual_rows):
        weighted = jnp.dot(dual_rows, matrix, precision=PRECISE)
        arrived = trade_blocks(pack_rows(weighted, target, total_slots), slot_depth)
        return variance * propagate(spread_rows(arrived, cell_index, field_shape), adjoint_weights)

    right_side = jnp.dot(innovations, matrix.T, precision=PRECISE) * is_live[:, None].astype(
        jnp.float32
    )
    solution = jnp.zeros_like(right_side)
    residual = right_side
    direction = right_side
    norm_now = squares(residual)
    for iter_index in range(ITERS):
        model_state = propagate(adjoint_spread(direction), forward_weights)
        returned = trade_blocks(sample_field(model_state, cell_index, total_slots), slot_depth)
        image = direction + jnp.dot(unpack_rows(returned, target), matrix.T, precision=PRECISE)
        step_size = norm_now / lax.psum(jnp.sum(direction * image), ("lat", "lon"))
        solution = solution + step_size * direction
        residual = residual - step_size * image
        norm_next = squares(residual)
        direction = residual + norm_next / norm_now * direction
        norm_now = norm_next
    return (solution, adjoint_spread(solution))


def solution(mesh):
    in_specs = (
        P(("lat", "lon"), None),
        P(("lat", "lon"), None),
        P(("lat", "lon")),
        P(("lat", "lon")),
        P(("lat", "lon")),
        P(("lat", "lon"), None, None),
        P(None, "lon", "lat"),
        P(None, "lon", "lat"),
        P(None, "lon", "lat"),
    )
    out_specs = (P(("lat", "lon"), None), P(None, "lon", "lat"))
    return jax.shard_map(body, mesh=mesh, in_specs=in_specs, out_specs=out_specs, check_vma=False)
```

profile of v0, /device:TPU:0, one launch (start us, length us, event | category | flops | bytes accessed | tf_op | source)
XLA Modules:
  0.0 1238.9 jit_solution(16313789601631541313)
XLA Ops:
  108.8 24.5 %scatter_custom_fusion.2 = f32[32,5120]{0,1:T(8,128)} fusion(s32[4096]{0:T(1024)S(1)} %bitcast.301, f32[4096,32]{1,0:T(8,128)} %bitcast.298, f32[]{:T(128)} %constant.13.clone.1), kind=kCustom, calls=%fused_computation.354 | custom fusion | flops 131072 | bytes 655872 | tf_op jit(solution)/shard_map/scatter-add | solution.py:91
  272.1 15.5 %fusion.132 = f32[32,40,128]{1,0,2:T(8,128)S(1)} fusion(f32[32,42,1]{1,0,2:T(8,128)S(1)} %collective-permute-done.19, f32[32,1,128]{1,0,2:T(8,128)} %copy.700, f32[32,40,128]{1,0,2:T(8,128)} %copy-done.24, f32[32,1,128]{1,0,2:T(8,128)} %copy.702, f32[32,42,1]{1,0,2:T(8,128)S(1)} %collective-permute-done.18, f32[32,40,128]{1,0,2:T(8,128)} %copy.665, ...), kind=kLoop, calls=%fused_computation.275 | loop fusion | flops 3112960 | bytes 5286400 | tf_op jit(solution)/shard_map/mul | solution.py:169
  336.8 13.2 %fusion.123 = f32[32,40,128]{1,0,2:T(8,128)S(1)} fusion(f32[32,42,1]{1,0,2:T(8,128)S(1)} %collective-permute-done.23, f32[32,1,128]{1,0,2:T(8,128)} %copy.707, f32[32,40,128]{1,0,2:T(8,128)} %copy-done.22, f32[32,1,128]{1,0,2:T(8,128)} %copy.710, f32[32,42,1]{1,0,2:T(8,128)S(1)} %collective-permute-done.22, f32[1,32,40,128]{2,1,3,0:T(8,128)} %copy.831, ...), kind=kLoop, calls=%fused_computation.258 | loop fusion | flops 2785280 | bytes 4631040 | tf_op jit(solution)/shard_map/add | solution.py:45
  376.9 11.5 fusion.115
  414.4 11.5 fusion.107
  452.1 12.3 fusion.99
  468.7 15.9 %gather_fusion = f32[4096,32]{1,0:T(8,128)} fusion(f32[32,5120]{0,1:T(8,128)} %bitcast.283, s32[4096]{0:T(1024)S(1)} %broadcast_clamp_fusion), kind=kCustom, calls=%fused_computation | custom fusion | bytes 1064960 | tf_op jit(solution)/shard_map/gather | solution.py:79
  499.3 16.3 %all-to-all-done.2 = f32[32,8,512]{2,1,0:T(8,128)} async-done(((f32[32,8,512]{2,1,0:T(8,128)}), f32[32,8,512]{2,1,0:T(8,128)}, u32[]{:S(2)}, u32[]{:S(2)}) %all-to-all-start.2) | async-done | bytes 524320 | tf_op jit(solution)/shard_map/all_to_all | solution.py:64
  523.6 37.5 %all-reduce.2 = (f32[]{:T(128)}, f32[]{:T(128)}) all-reduce(f32[]{:T(128)} %get-tuple-element.13, f32[]{:T(128)} %get-tuple-element.12), channel_id=1, replica_groups=mesh['lat'=4,'lon'=8] {'lat','lon'}, use_global_device_ids=true, to_apply=%region_1.2 | all-reduce | flops 2 | bytes 16 | tf_op jit(solution)/shard_map/psum | solution.py:97
  564.1 41.5 %psum.30 = f32[]{:T(128)} all-reduce(f32[]{:T(128)} %multiply_reduce_fusion), channel_id=1, replica_groups=mesh['lat'=4,'lon'=8] {'lat','lon'}, use_global_device_ids=true, to_apply=%region_10.11 | all-reduce | flops 1 | bytes 8 | tf_op jit(solution)/shard_map/psum | solution.py:97
  612.5 21.5 %all_to_all.30 = f32[32,8,512]{2,1,0:T(8,128)} all-to-all(f32[32,8,512]{2,1,0:T(8,128)S(1)} %slice_bitcast_fusion.6), channel_id=1, replica_groups=mesh['lat'=4,'lon'=8] {'lat','lon'}, dimensions={0} | all-to-all | bytes 1048576 | tf_op jit(solution)/shard_map/all_to_all | solution.py:64
  641.6 24.3 %scatter_custom_fusion.4 = f32[32,5120]{0,1:T(8,128)} fusion(s32[4096]{0:T(1024)S(1)} %bitcast.303, f32[4096,32]{1,0:T(8,128)} %bitcast.299, f32[]{:T(128)} %constant.13.clone.1), kind=kCustom, calls=%fused_computation.352 | custom fusion | flops 131072 | bytes 655872 | tf_op jit(solution)/shard_map/scatter-add | solution.py:91
  794.8 10.8 fusion.67
  831.8 11.5 fusion.58
  869.6 11.5 fusion.50
  907.6 11.5 fusion.42
  945.3 12.5 %fusion.34 = f32[32,40,128]{1,0,2:T(8,128)} fusion(f32[32,42,1]{1,0,2:T(8,128)S(1)} %collective-permute-done.67, f32[32,1,128]{1,0,2:T(8,128)} %copy.783, f32[32,40,128]{1,0,2:T(8,128)} %copy-done.23, f32[32,1,128]{1,0,2:T(8,128)} %copy.785, f32[32,42,1]{1,0,2:T(8,128)S(1)} %collective-permute-done.66, f32[1,32,40,128]{2,1,3,0:T(8,128)} %copy.831, ...), kind=kLoop, calls=%fused_computation.81 | loop fusion | flops 2785280 | bytes 4631040 | tf_op jit(solution)/shard_map/add | solution.py:45
  962.2 12.5 %gather_fusion.2 = f32[4096,32]{1,0:T(8,128)S(1)} fusion(f32[32,5120]{0,1:T(8,128)} %bitcast.282, s32[4096]{0:T(1024)S(1)} %broadcast_clamp_fusion), kind=kCustom, calls=%fused_computation.2 | custom fusion | bytes 1064960 | tf_op jit(solution)/shard_map/gather | solution.py:79
  982.0 21.7 %all_to_all.31 = f32[32,8,512]{2,1,0:T(8,128)S(1)} all-to-all(f32[32,8,512]{2,1,0:T(8,128)S(1)} %reshape_reshape.18), channel_id=1, replica_groups=mesh['lat'=4,'lon'=8] {'lat','lon'}, dimensions={0} | all-to-all | bytes 1048576 | tf_op jit(solution)/shard_map/all_to_all | solution.py:64
  1006.4 37.4 %psum.31 = f32[]{:T(128)} all-reduce(f32[]{:T(128)} %fusion.179), channel_id=1, replica_groups=mesh['lat'=4,'lon'=8] {'lat','lon'}, use_global_device_ids=true, to_apply=%region_14.15 | all-reduce | flops 1 | bytes 8 | tf_op jit(solution)/shard_map/psum | solution.py:182
  1047.3 21.0 %all_to_all.32 = f32[32,8,512]{2,1,0:T(8,128)S(1)} all-to-all(f32[32,8,512]{2,1,0:T(8,128)S(1)} %slice_bitcast_fusion.5), channel_id=1, replica_groups=mesh['lat'=4,'lon'=8] {'lat','lon'}, dimensions={0} | all-to-all | bytes 1048576 | tf_op jit(solution)/shard_map/all_to_all | solution.py:64
  1073.9 24.1 %scatter_custom_fusion.6 = f32[32,5120]{0,1:T(8,128)} fusion(s32[4096]{0:T(1024)} %bitcast.304, f32[4096,32]{1,0:T(8,128)S(1)} %bitcast.297, f32[]{:T(128)} %constant.13.clone.1), kind=kCustom, calls=%fused_computation.350 | custom fusion | flops 131072 | bytes 655872 | tf_op jit(solution)/shard_map/scatter-add | solution.py:91
  1116.5 11.6 fusion.26
  1224.3 10.6 fusion.2
  (565 shorter events, 789.0 us)
Async XLA Ops:
  4.9 25.0 %collective-permute-start = (f32[160,5,128]{2,0,1:T(8,128)S(1)}, f32[160,5,128]{2,0,1:T(8,128)S(1)}, u32[]{:S(2)}, u32[]{:S(2)}) collective-permute-start(f32[160,5,128]{2,0,1:T(8,128)S(1)} %get-tuple-element.68), channel_id=1, source_target_pairs={{0,1},{1,2},{2,3},{3,4},{4,5},{5,6},{6,7},{7,0},{8,9},{9,10},{10,1... | collective-permute-start | bytes 1228808 | tf_op jit(solution)/shard_map/ppermute | solution.py:23
  5.4 24.5 %collective-permute-start.1 = (f32[160,5,128]{2,0,1:T(8,128)S(1)}, f32[160,5,128]{2,0,1:T(8,128)S(1)}, u32[]{:S(2)}, u32[]{:S(2)}) collective-permute-start(f32[160,5,128]{2,0,1:T(8,128)S(1)} %get-tuple-element.69), channel_id=1, source_target_pairs={{1,0},{2,1},{3,2},{4,3},{5,4},{6,5},{7,6},{0,7},{9,8},{10,9},{11,1... | collective-permute-start | bytes 1228808 | tf_op jit(solution)/shard_map/ppermute | solution.py:24
  12.6 11.7 all-to-all-start
  24.3 76.8 %all-to-all-start.1 = ((f32[32,8,512]{2,1,0:T(8,128)}), f32[32,8,512]{2,1,0:T(8,128)}, u32[]{:S(2)}, u32[]{:S(2)}) async-start(f32[32,8,512]{2,1,0:T(8,128)} %slice_bitcast_fusion.7), calls=%async_computation.1 | async-start | bytes 1048576 | tf_op jit(solution)/shard_map/all_to_all | solution.py:64
  41.4 10.0 collective-permute-start.2
  49.2 10.5 collective-permute-start.3
  136.2 7.1 collective-permute-start.5
  147.1 15.7 %collective-permute-start.6 = (f32[32,42,1]{1,0,2:T(8,128)S(1)}, f32[32,42,1]{1,0,2:T(8,128)S(1)}, u32[]{:S(2)}, u32[]{:S(2)}) collective-permute-start(f32[32,42,1]{1,0,2:T(8,128)S(1)} %get-tuple-element.64), channel_id=1, source_target_pairs={{8,0},{16,8},{24,16},{9,1},{17,9},{25,17},{10,2},{18,10},{26,18},{... | collective-permute-start | bytes 16136 | tf_op jit(solution)/shard_map/ppermute | solution.py:24
  148.4 14.3 %collective-permute-start.7 = (f32[32,42,1]{1,0,2:T(8,128)S(1)}, f32[32,42,1]{1,0,2:T(8,128)S(1)}, u32[]{:S(2)}, u32[]{:S(2)}) collective-permute-start(f32[32,42,1]{1,0,2:T(8,128)S(1)} %get-tuple-element.65), channel_id=1, source_target_pairs={{0,8},{8,16},{16,24},{1,9},{9,17},{17,25},{2,10},{10,18},{18,26},{... | collective-permute-start | bytes 16136 | tf_op jit(solution)/shard_map/ppermute | solution.py:23
  261.3 10.8 collective-permute-start.18
  262.6 9.5 collective-permute-start.19
  305.6 31.2 %collective-permute-start.22 = (f32[32,42,1]{1,0,2:T(8,128)S(1)}, f32[32,42,1]{1,0,2:T(8,128)S(1)}, u32[]{:S(2)}, u32[]{:S(2)}) collective-permute-start(f32[32,42,1]{1,0,2:T(8,128)S(1)} %get-tuple-element.56), channel_id=1, source_target_pairs={{8,0},{16,8},{24,16},{9,1},{17,9},{25,17},{10,2},{18,10},{26,18},{... | collective-permute-start | bytes 16136 | tf_op jit(solution)/shard_map/ppermute | solution.py:24
  306.9 29.9 %collective-permute-start.23 = (f32[32,42,1]{1,0,2:T(8,128)S(1)}, f32[32,42,1]{1,0,2:T(8,128)S(1)}, u32[]{:S(2)}, u32[]{:S(2)}) collective-permute-start(f32[32,42,1]{1,0,2:T(8,128)S(1)} %get-tuple-element.57), channel_id=1, source_target_pairs={{0,8},{8,16},{16,24},{1,9},{9,17},{17,25},{2,10},{10,18},{18,26},{... | collective-permute-start | bytes 16136 | tf_op jit(solution)/shard_map/ppermute | solution.py:23
  406.2 6.9 collective-permute-start.30
  443.6 7.2 collective-permute-start.34
  493.6 22.0 %all-to-all-start.2 = ((f32[32,8,512]{2,1,0:T(8,128)}), f32[32,8,512]{2,1,0:T(8,128)}, u32[]{:S(2)}, u32[]{:S(2)}) async-start(f32[32,8,512]{2,1,0:T(8,128)} %reshape_reshape.16), calls=%async_computation.2 | async-start | bytes 1048576 | tf_op jit(solution)/shard_map/all_to_all | solution.py:64
  750.5 7.0 collective-permute-start.46
  786.4 7.4 collective-permute-start.50
  823.4 7.2 collective-permute-start.54
  861.1 7.0 collective-permute-start.58
  899.1 7.0 collective-permute-start.62
  936.9 7.4 collective-permute-start.66
  1180.2 7.3 collective-permute-start.78
  1215.8 7.3 collective-permute-start.82
  (151 other events, 2270.7 us)
where the time goes:
time: 1250 us; the launch traced here: 1240 us
  local copies, waits for them, and re-layouts  438 us (35%)
  other arithmetic  337 us (27%)
  starting transfers between devices  184 us (15%)
  blocking collectives  181 us (14%)
  waiting for transfers between devices  81 us (6%)
    add x17, other arithmetic, stencil(): local_weights[0] * padded[:, 1:-1, 1:-1]  184 us
    ppermute x42, starting transfers between devices, with_halo(): before = lax.ppermute(last, axis, up)  112 us
    slice x40, local copies, waits for them, and re-layouts, with_halo(): last = lax.slice_in_dim(array, length - width, length, axis=dim)  101 us
    psum x2, blocking collectives, squares(): return lax.psum(jnp.sum(residual * residual), ('lat', 'lon'))  78.9 us
    scatter-add x3, other arithmetic, spread_rows(): flat_field = jnp.zeros((LEV, field_shape[1] * field_shape[2]), jnp.float3...  72.8 us
    all_to_all x3, blocking collectives, trade_blocks(): lax.all_to_all(direct, ('lat', 'lon'), split_axis=0, concat_axis=0, tiled...  64.2 us
    ppermute x21, local copies, waits for them, and re-layouts, with_halo(): before = lax.ppermute(last, axis, up)  61 us
    ppermute x21, local copies, waits for them, and re-layouts, with_halo(): after = lax.ppermute(leading, axis, down)  60.2 us
  transfers between devices with their start and end apart: 87, of which 39 were waited for; matrix products, arithmetic and copies ran while one was open for 17% of the time, Pallas kernels for 0%

commit v1 on v0

--- a/solution.py
+++ b/solution.py
@@ -163,29 +163,30 @@
     )
     variance = background_std * background_std
 
-    def adjoint_spread(dual_rows):
+    def propagate_rows(dual_rows):
         weighted = jnp.dot(dual_rows, matrix, precision=PRECISE)
         arrived = trade_blocks(pack_rows(weighted, target, total_slots), slot_depth)
-        return variance * propagate(spread_rows(arrived, cell_index, field_shape), adjoint_weights)
+        return propagate(spread_rows(arrived, cell_index, field_shape), adjoint_weights)
 
     right_side = jnp.dot(innovations, matrix.T, precision=PRECISE) * is_live[:, None].astype(
         jnp.float32
     )
-    solution = jnp.zeros_like(right_side)
-    residual = right_side
-    direction = right_side
-    norm_now = squares(residual)
-    for iter_index in range(ITERS):
-        model_state = propagate(adjoint_spread(direction), forward_weights)
-        returned = trade_blocks(sample_field(model_state, cell_index, total_slots), slot_depth)
-        image = direction + jnp.dot(unpack_rows(returned, target), matrix.T, precision=PRECISE)
-        step_size = norm_now / lax.psum(jnp.sum(direction * image), ("lat", "lon"))
-        solution = solution + step_size * direction
-        residual = residual - step_size * image
-        norm_next = squares(residual)
-        direction = residual + norm_next / norm_now * direction
-        norm_now = norm_next
-    return (solution, adjoint_spread(solution))
+    norm_first = squares(right_side)
+    first = propagate_rows(right_side)
+    energy = jnp.sum(first * variance * first)
+    step_first = norm_first / (norm_first + lax.psum(energy, ("lat", "lon")))
+    model_state = propagate(variance * first, forward_weights)
+    returned = trade_blocks(sample_field(model_state, cell_index, total_slots), slot_depth)
+    image = right_side + jnp.dot(unpack_rows(returned, target), matrix.T, precision=PRECISE)
+    residual = right_side - step_first * image
+    norm_next = squares(residual)
+    ratio = norm_next / norm_first
+    direction = residual + ratio * right_side
+    second = propagate_rows(residual) + ratio * first
+    energy = jnp.sum(direction * direction) + jnp.sum(second * variance * second)
+    step_second = norm_next / lax.psum(energy, ("lat", "lon"))
+    solution = step_first * right_side + step_second * direction
+    return (solution, variance * (step_first * first + step_second * second))
 
 
 def solution(mesh):

time: 1250 us -> 857 us (0.69)
  local copies, waits for them, and re-layouts: 438 us -> 302 us
  other arithmetic: 337 us -> 228 us
  starting transfers between devices: 184 us -> 120 us
  waiting for transfers between devices: 81 us -> 37 us
  blocking collectives: 181 us -> 146 us
    add x17 -> x10, other arithmetic: 184 us -> 108 us  [stencil(): local_weights[0] * padded[:, 1:-1, 1:-1]]
    ppermute x42 -> x26, starting transfers between devices: 112 us -> 68.5 us  [with_halo(): before = lax.ppermute(last, axis, up)]
    all_to_all x3 -> x1, blocking collectives: 64.2 us -> 21.5 us  [trade_blocks(): lax.all_to_all(direct, ('lat', 'lon'), split_axis=0, concat_axis=0, tiled...]
    slice x40 -> x25, local copies, waits for them, and re-layouts: 101 us -> 63.8 us  [with_halo(): last = lax.slice_in_dim(array, length - width, length, axis=dim)]
    mul x3 -> x2, other arithmetic: 36.9 us -> 4.81 us  [the longest x1 4.32 us: body(): return (solution, variance * (step_first * first + step_second * second))]
    reduce_sum x1 -> x3, other arithmetic: 1.63 us -> 30.2 us  [the longest x1 16.1 us: body(): energy = jnp.sum(first * variance * first)]
    ppermute x42 -> x26, waiting for transfers between devices: 57.6 us -> 29.2 us  [with_halo(): before = lax.ppermute(last, axis, up)]
    scatter-add x3 -> x2, other arithmetic: 72.8 us -> 48.8 us  [spread_rows(): flat_field = jnp.zeros((LEV, field_shape[1] * field_shape[2]), jnp.float3...]
  transfers between devices with their start and end apart: 87 -> 55, of which waited for: 39 -> 19; matrix products, arithmetic and copies ran while one was open for 17% -> 21% of each run, Pallas kernels for 0% -> 0%
where the time goes in v1:
time: 857 us; the launch traced here: 848 us
  local copies, waits for them, and re-layouts  302 us (35%)
  other arithmetic  228 us (27%)
  blocking collectives  146 us (17%)
  starting transfers between devices  120 us (14%)
  waiting for transfers between devices  37 us (4%)
  between operations  8.78 us (1%)
    add x10, other arithmetic, stencil(): local_weights[0] * padded[:, 1:-1, 1:-1]  108 us
    psum x2, blocking collectives, squares(): return lax.psum(jnp.sum(residual * residual), ('lat', 'lon'))  82.6 us
    ppermute x26, starting transfers between devices, with_halo(): before = lax.ppermute(last, axis, up)  68.5 us
    slice x25, local copies, waits for them, and re-layouts, with_halo(): last = lax.slice_in_dim(array, length - width, length, axis=dim)  63.8 us
    unnamed x141, local copies, waits for them, and re-layouts  56.6 us
    scatter-add x2, other arithmetic, spread_rows(): flat_field = jnp.zeros((LEV, field_shape[1] * field_shape[2]), jnp.float3...  48.8 us
    psum x1, blocking collectives, body(): step_second = norm_next / lax.psum(energy, ('lat', 'lon'))  42 us
    ppermute x13, local copies, waits for them, and re-layouts, with_halo(): after = lax.ppermute(leading, axis, down)  38.1 us
  transfers between devices with their start and end apart: 55, of which 19 were waited for; matrix products, arithmetic and copies ran while one was open for 21% of the time, Pallas kernels for 0%

profile of v1, /device:TPU:0, one launch (start us, length us, event | category | flops | bytes accessed | tf_op | source)
XLA Modules:
  0.0 847.7 jit_solution(4583411300343332530)
XLA Ops:
  63.7 7.6 pad_maximum_fusion
  108.5 24.4 %scatter_custom_fusion.2 = f32[32,5120]{0,1:T(8,128)} fusion(s32[4096]{0:T(1024)S(1)} %bitcast.217, f32[4096,32]{1,0:T(8,128)S(1)} %bitcast.216, f32[]{:T(128)} %constant.13.clone.1), kind=kCustom, calls=%fused_computation.219 | custom fusion | flops 131072 | bytes 655364 | tf_op jit(solution)/shard_map/scatter-add | solution.py:91
  154.8 9.1 %broadcast_multiply_fusion = f32[5,32,48,136]{2,1,3,0:T(8,128)} fusion(f32[5,32,48,136]{2,1,3,0:T(8,128)} %constant_dynamic-update-slice_fusion, f32[136]{0:T(256)S(1)} %copy-done.57), kind=kLoop, calls=%fused_computation.8 | loop fusion | flops 1044480 | bytes 8356384 | tf_op jit(solution)/shard_map/mul | solution.py:153
  164.0 9.5 %fusion.91 = f32[32,40,128]{1,0,2:T(8,128)S(1)} fusion(f32[32,42,1]{1,0,2:T(8,128)S(1)} %collective-permute-done.7, f32[32,1,128]{1,0,2:T(8,128)S(1)} %copy-done.32, f32[32,40,128]{1,0,2:T(8,128)S(1)} %copy-done.29, f32[32,1,128]{1,0,2:T(8,128)S(1)} %copy-done.38, f32[32,42,1]{1,0,2:T(8,128)S(1)} %collective-permute-done.6, ...), kind=kLoop, calls=%fused_computation.191 | loop fusion | flops 2785280 | bytes 4631040 | tf_op jit(solution)/shard_map/add | solution.py:45
  201.8 9.6 %fusion.83 = f32[32,40,128]{1,0,2:T(8,128)S(1)} fusion(f32[32,42,1]{1,0,2:T(8,128)S(1)} %collective-permute-done.11, f32[32,1,128]{1,0,2:T(8,128)S(1)} %copy-done.33, f32[32,40,128]{1,0,2:T(8,128)S(1)} %fusion.91, f32[32,1,128]{1,0,2:T(8,128)S(1)} %copy-done.39, f32[32,42,1]{1,0,2:T(8,128)S(1)} %collective-permute-done.10, ...), kind=kLoop, calls=%fused_computation.175 | loop fusion | flops 2785280 | bytes 4631040 | tf_op jit(solution)/shard_map/add | solution.py:45
  235.3 9.6 %fusion.75 = f32[32,40,128]{1,0,2:T(8,128)S(1)} fusion(f32[32,42,1]{1,0,2:T(8,128)S(1)} %collective-permute-done.15, f32[32,1,128]{1,0,2:T(8,128)S(1)} %copy-done.34, f32[32,40,128]{1,0,2:T(8,128)S(1)} %copy-done.17, f32[32,1,128]{1,0,2:T(8,128)S(1)} %copy-done.40, f32[32,42,1]{1,0,2:T(8,128)S(1)} %collective-permute-done.14, ...), kind=kLoop, calls=%fused_computation.159 | loop fusion | flops 2785280 | bytes 4631040 | tf_op jit(solution)/shard_map/add | solution.py:45
  263.6 5.8 collective-permute-start.19
  272.4 16.1 %multiply_reduce_fusion = (f32[]{:T(128)}, f32[32,40,128]{1,0,2:T(8,128)S(1)}) fusion(f32[32,40,128]{1,0,2:T(8,128)S(1)} %copy.483, f32[32,1,128]{1,0,2:T(8,128)} %copy.478, f32[32,40,128]{1,0,2:T(8,128)} %copy-done.14, f32[32,1,128]{1,0,2:T(8,128)} %copy.480, f32[32,42,1]{1,0,2:T(8,128)S(1)} %collective-permute-done.19, ...), kind=kLoop, calls=%fused_computation.215 | loop fusion | flops 3440639 | bytes 5286404 | tf_op jit(solution)/shard_map/reduce_sum | solution.py:176
  309.1 5.6 collective-permute-start.23
  339.9 14.3 %fusion.59 = f32[32,40,128]{1,0,2:T(8,128)S(1)} fusion(f32[32,42,1]{1,0,2:T(8,128)S(1)} %collective-permute-done.23, f32[32,1,128]{1,0,2:T(8,128)} %copy.488, f32[32,40,128]{1,0,2:T(8,128)} %copy-done.10, f32[32,1,128]{1,0,2:T(8,128)} %copy.491, f32[32,42,1]{1,0,2:T(8,128)S(1)} %collective-permute-done.22, f32[1,32,40,128]{2,1,3,0:T(8,128)} %copy.557, ...), kind=kLoop, calls=%fused_computation.127 | loop fusion | flops 2785280 | bytes 4631040 | tf_op jit(solution)/shard_map/add | solution.py:45
  380.8 11.6 %fusion.51 = f32[32,40,128]{1,0,2:T(8,128)S(1)} fusion(f32[32,42,1]{1,0,2:T(8,128)S(1)} %collective-permute-done.27, f32[32,1,128]{1,0,2:T(8,128)} %copy.497, f32[32,40,128]{1,0,2:T(8,128)} %copy-done.18, f32[32,1,128]{1,0,2:T(8,128)} %copy.499, f32[32,42,1]{1,0,2:T(8,128)S(1)} %collective-permute-done.26, f32[1,32,40,128]{2,1,3,0:T(8,128)} %copy.557, ...), kind=kLoop, calls=%fused_computation.111 | loop fusion | flops 2785280 | bytes 4631040 | tf_op jit(solution)/shard_map/add | solution.py:45
  418.3 11.6 %fusion.43 = f32[32,40,128]{1,0,2:T(8,128)S(1)} fusion(f32[32,42,1]{1,0,2:T(8,128)S(1)} %collective-permute-done.31, f32[32,1,128]{1,0,2:T(8,128)} %copy.503, f32[32,40,128]{1,0,2:T(8,128)} %copy-done.19, f32[32,1,128]{1,0,2:T(8,128)} %copy.505, f32[32,42,1]{1,0,2:T(8,128)S(1)} %collective-permute-done.30, f32[1,32,40,128]{2,1,3,0:T(8,128)} %copy.557, ...), kind=kLoop, calls=%fused_computation.95 | loop fusion | flops 2785280 | bytes 4631040 | tf_op jit(solution)/shard_map/add | solution.py:45
  456.0 12.6 %fusion.35 = f32[32,40,128]{1,0,2:T(8,128)} fusion(f32[32,42,1]{1,0,2:T(8,128)S(1)} %collective-permute-done.35, f32[32,1,128]{1,0,2:T(8,128)} %copy.509, f32[32,40,128]{1,0,2:T(8,128)} %copy-done.13, f32[32,1,128]{1,0,2:T(8,128)} %copy.511, f32[32,42,1]{1,0,2:T(8,128)S(1)} %collective-permute-done.34, f32[1,32,40,128]{2,1,3,0:T(8,128)} %copy.557, ...), kind=kLoop, calls=%fused_computation.79 | loop fusion | flops 2785280 | bytes 4631040 | tf_op jit(solution)/shard_map/add | solution.py:45
  472.8 15.8 %gather_fusion = f32[4096,32]{1,0:T(8,128)} fusion(f32[32,5120]{0,1:T(8,128)} %bitcast.206, s32[4096]{0:T(1024)S(1)} %broadcast_clamp_fusion), kind=kCustom, calls=%fused_computation | custom fusion | bytes 1064960 | tf_op jit(solution)/shard_map/gather | solution.py:79
  497.6 5.7 all-to-all-start.2
  503.3 40.8 %all-reduce.1 = (f32[]{:T(128)}, f32[]{:T(128)}) all-reduce(f32[]{:T(128)} %get-tuple-element.82, f32[]{:T(128)} %get-tuple-element.16), channel_id=1, replica_groups=mesh['lat'=4,'lon'=8] {'lat','lon'}, use_global_device_ids=true, to_apply=%region_1.2 | all-reduce | flops 2 | bytes 16 | tf_op jit(solution)/shard_map/psum | solution.py:97
  558.9 21.5 %all_to_all.20 = f32[32,8,512]{2,1,0:T(8,128)} all-to-all(f32[32,8,512]{2,1,0:T(8,128)S(1)} %slice_bitcast_fusion.5), channel_id=1, replica_groups=mesh['lat'=4,'lon'=8] {'lat','lon'}, dimensions={0} | all-to-all | bytes 1048576 | tf_op jit(solution)/shard_map/all_to_all | solution.py:64
  588.0 24.4 %scatter_custom_fusion.4 = f32[32,5120]{0,1:T(8,128)} fusion(s32[4096]{0:T(1024)S(1)} %bitcast.219, f32[4096,32]{1,0:T(8,128)} %bitcast.215, f32[]{:T(128)} %constant.13.clone.1), kind=kCustom, calls=%fused_computation.217 | custom fusion | flops 131072 | bytes 655872 | tf_op jit(solution)/shard_map/scatter-add | solution.py:91
  631.8 9.6 %fusion.27 = f32[32,40,128]{1,0,2:T(8,128)S(1)} fusion(f32[32,42,1]{1,0,2:T(8,128)S(1)} %collective-permute-done.39, f32[32,1,128]{1,0,2:T(8,128)S(1)} %copy-done.35, f32[32,40,128]{1,0,2:T(8,128)S(1)} %copy-done.30, f32[32,1,128]{1,0,2:T(8,128)S(1)} %copy-done.41, f32[32,42,1]{1,0,2:T(8,128)S(1)} %collective-permute-done.38, ...), kind=kLoop, calls=%fused_computation.63 | loop fusion | flops 2785280 | bytes 4631040 | tf_op jit(solution)/shard_map/add | solution.py:45
  668.7 9.6 %fusion.19 = f32[32,40,128]{1,0,2:T(8,128)S(1)} fusion(f32[32,42,1]{1,0,2:T(8,128)S(1)} %collective-permute-done.43, f32[32,1,128]{1,0,2:T(8,128)S(1)} %copy-done.36, f32[32,40,128]{1,0,2:T(8,128)S(1)} %copy-done.21, f32[32,1,128]{1,0,2:T(8,128)S(1)} %copy-done.42, f32[32,42,1]{1,0,2:T(8,128)S(1)} %collective-permute-done.42, ...), kind=kLoop, calls=%fused_computation.47 | loop fusion | flops 2785280 | bytes 4631040 | tf_op jit(solution)/shard_map/add | solution.py:45
  704.3 9.6 %fusion.11 = f32[32,40,128]{1,0,2:T(8,128)S(1)} fusion(f32[32,42,1]{1,0,2:T(8,128)S(1)} %collective-permute-done.47, f32[32,1,128]{1,0,2:T(8,128)S(1)} %copy-done.37, f32[32,40,128]{1,0,2:T(8,128)S(1)} %copy-done.23, f32[32,1,128]{1,0,2:T(8,128)S(1)} %copy-done.43, f32[32,42,1]{1,0,2:T(8,128)S(1)} %collective-permute-done.46, ...), kind=kLoop, calls=%fused_computation.31 | loop fusion | flops 2785280 | bytes 4631040 | tf_op jit(solution)/shard_map/add | solution.py:45
  722.6 41.8 %psum.30 = f32[]{:T(128)} all-reduce(f32[]{:T(128)} %get-tuple-element.84), channel_id=1, replica_groups=mesh['lat'=4,'lon'=8] {'lat','lon'}, use_global_device_ids=true, to_apply=%region_10.11 | all-reduce | flops 1 | bytes 8 | tf_op jit(solution)/shard_map/psum | solution.py:97
  780.8 12.4 %fusion = (f32[]{:T(128)}, f32[32,40,128]{1,0,2:T(8,128)}) fusion(f32[32,40,128]{1,0,2:T(8,128)S(1)} %copy.483, f32[32,40,128]{1,0,2:T(8,128)S(1)} %copy-done.27, f32[]{:T(128)S(6)} %div.10, f32[32,1,128]{1,0,2:T(8,128)S(1)} %copy-done.31, f32[32,40,128]{1,0,2:T(8,128)S(1)} %copy-done.12, f32[32,1,128]{1,0,2:T(8,128)} %copy.542, ...), kind=kLoop, calls=%fused_computation.11 | loop fusion | flops 3768319 | bytes 5941768 | tf_op jit(solution)/shard_map/reduce_sum | solution.py:186
  794.6 42.0 %psum.31 = f32[]{:T(128)} all-reduce(f32[]{:T(128)S(6)} %add.342), channel_id=1, replica_groups=mesh['lat'=4,'lon'=8] {'lat','lon'}, use_global_device_ids=true, to_apply=%region_15.16 | all-reduce | flops 1 | bytes 8 | tf_op jit(solution)/shard_map/psum | solution.py:187
  (375 shorter events, 458.0 us)
Async XLA Ops:
  5.8 24.2 %collective-permute-start = (f32[160,5,128]{2,0,1:T(8,128)}, f32[160,5,128]{2,0,1:T(8,128)S(1)}, u32[]{:S(2)}, u32[]{:S(2)}) collective-permute-start(f32[160,5,128]{2,0,1:T(8,128)} %get-tuple-element.54), channel_id=1, source_target_pairs={{0,1},{1,2},{2,3},{3,4},{4,5},{5,6},{6,7},{7,0},{8,9},{9,10},{10,1... | collective-permute-start | bytes 1228808 | tf_op jit(solution)/shard_map/ppermute | solution.py:23
  6.2 23.8 %collective-permute-start.1 = (f32[160,5,128]{2,0,1:T(8,128)}, f32[160,5,128]{2,0,1:T(8,128)S(1)}, u32[]{:S(2)}, u32[]{:S(2)}) collective-permute-start(f32[160,5,128]{2,0,1:T(8,128)} %get-tuple-element.55), channel_id=1, source_target_pairs={{1,0},{2,1},{3,2},{4,3},{5,4},{6,5},{7,6},{0,7},{9,8},{10,9},{11,1... | collective-permute-start | bytes 1228808 | tf_op jit(solution)/shard_map/ppermute | solution.py:24
  13.3 11.8 %all-to-all-start = ((s32[32,8,2]{1,2,0:T(2,128)}), s32[32,8,2]{1,2,0:T(2,128)S(1)}, u32[]{:S(2)}, u32[]{:S(2)}) async-start(s32[32,8,2]{1,2,0:T(2,128)} %copy.451), calls=%async_computation | async-start | bytes 65536 | tf_op jit(solution)/shard_map/all_to_all | solution.py:126
  25.1 77.8 %all-to-all-start.1 = ((f32[32,8,512]{2,1,0:T(8,128)}), f32[32,8,512]{2,1,0:T(8,128)S(1)}, u32[]{:S(2)}, u32[]{:S(2)}) async-start(f32[32,8,512]{2,1,0:T(8,128)} %slice_bitcast_fusion.6), calls=%async_computation.1 | async-start | bytes 1048576 | tf_op jit(solution)/shard_map/all_to_all | solution.py:64
  41.3 10.1 %collective-permute-start.2 = (f32[160,50,5]{0,1,2:T(8,128)S(1)}, f32[160,50,5]{0,1,2:T(8,128)S(1)}, u32[]{:S(2)}, u32[]{:S(2)}) collective-permute-start(f32[160,50,5]{0,1,2:T(8,128)S(1)} %copy.441), channel_id=1, source_target_pairs={{0,8},{8,16},{16,24},{1,9},{9,17},{17,25},{2,10},{10,18},{18,26},{... | collective-permute-start | bytes 480008 | tf_op jit(solution)/shard_map/ppermute | solution.py:23
  49.3 10.6 %collective-permute-start.3 = (f32[160,50,5]{0,1,2:T(8,128)S(1)}, f32[160,50,5]{0,1,2:T(8,128)}, u32[]{:S(2)}, u32[]{:S(2)}) collective-permute-start(f32[160,50,5]{0,1,2:T(8,128)S(1)} %copy.442), channel_id=1, source_target_pairs={{8,0},{16,8},{24,16},{9,1},{17,9},{25,17},{10,2},{18,10},{26,18},{... | collective-permute-start | bytes 480008 | tf_op jit(solution)/shard_map/ppermute | solution.py:24
  133.8 7.9 collective-permute-start.4
  135.8 8.7 %collective-permute-start.5 = (f32[32,1,128]{2,0,1:T(8,128)S(1)}, f32[32,1,128]{2,0,1:T(8,128)S(1)}, u32[]{:S(2)}, u32[]{:S(2)}) collective-permute-start(f32[32,1,128]{2,0,1:T(8,128)S(1)} %copy.552), channel_id=1, source_target_pairs={{0,1},{1,2},{2,3},{3,4},{4,5},{5,6},{6,7},{7,0},{8,9},{9,10},{10,1... | collective-permute-start | bytes 49160 | tf_op jit(solution)/shard_map/ppermute | solution.py:23
  148.3 15.6 %collective-permute-start.6 = (f32[32,42,1]{1,0,2:T(8,128)S(1)}, f32[32,42,1]{1,0,2:T(8,128)S(1)}, u32[]{:S(2)}, u32[]{:S(2)}) collective-permute-start(f32[32,42,1]{1,0,2:T(8,128)S(1)} %get-tuple-element.50), channel_id=1, source_target_pairs={{8,0},{16,8},{24,16},{9,1},{17,9},{25,17},{10,2},{18,10},{26,18},{... | collective-permute-start | bytes 16136 | tf_op jit(solution)/shard_map/ppermute | solution.py:24
  149.6 14.3 %collective-permute-start.7 = (f32[32,42,1]{1,0,2:T(8,128)S(1)}, f32[32,42,1]{1,0,2:T(8,128)S(1)}, u32[]{:S(2)}, u32[]{:S(2)}) collective-permute-start(f32[32,42,1]{1,0,2:T(8,128)S(1)} %get-tuple-element.51), channel_id=1, source_target_pairs={{0,8},{8,16},{16,24},{1,9},{9,17},{17,25},{2,10},{10,18},{18,26},{... | collective-permute-start | bytes 16136 | tf_op jit(solution)/shard_map/ppermute | solution.py:23
  262.3 10.1 %collective-permute-start.18 = (f32[32,42,1]{1,0,2:T(8,128)S(1)}, f32[32,42,1]{1,0,2:T(8,128)S(1)}, u32[]{:S(2)}, u32[]{:S(2)}) collective-permute-start(f32[32,42,1]{1,0,2:T(8,128)S(1)} %get-tuple-element.44), channel_id=1, source_target_pairs={{8,0},{16,8},{24,16},{9,1},{17,9},{25,17},{10,2},{18,10},{26,18},{... | collective-permute-start | bytes 16136 | tf_op jit(solution)/shard_map/ppermute | solution.py:24
  263.6 8.8 %collective-permute-start.19 = (f32[32,42,1]{1,0,2:T(8,128)S(1)}, f32[32,42,1]{1,0,2:T(8,128)S(1)}, u32[]{:S(2)}, u32[]{:S(2)}) collective-permute-start(f32[32,42,1]{1,0,2:T(8,128)S(1)} %get-tuple-element.45), channel_id=1, source_target_pairs={{0,8},{8,16},{16,24},{1,9},{9,17},{17,25},{2,10},{10,18},{18,26},{... | collective-permute-start | bytes 16136 | tf_op jit(solution)/shard_map/ppermute | solution.py:23
  307.8 32.1 %collective-permute-start.22 = (f32[32,42,1]{1,0,2:T(8,128)S(1)}, f32[32,42,1]{1,0,2:T(8,128)S(1)}, u32[]{:S(2)}, u32[]{:S(2)}) collective-permute-start(f32[32,42,1]{1,0,2:T(8,128)S(1)} %get-tuple-element.42), channel_id=1, source_target_pairs={{8,0},{16,8},{24,16},{9,1},{17,9},{25,17},{10,2},{18,10},{26,18},{... | collective-permute-start | bytes 16136 | tf_op jit(solution)/shard_map/ppermute | solution.py:24
  309.1 30.8 %collective-permute-start.23 = (f32[32,42,1]{1,0,2:T(8,128)S(1)}, f32[32,42,1]{1,0,2:T(8,128)S(1)}, u32[]{:S(2)}, u32[]{:S(2)}) collective-permute-start(f32[32,42,1]{1,0,2:T(8,128)S(1)} %get-tuple-element.43), channel_id=1, source_target_pairs={{0,8},{8,16},{16,24},{1,9},{9,17},{17,25},{2,10},{10,18},{18,26},{... | collective-permute-start | bytes 16136 | tf_op jit(solution)/shard_map/ppermute | solution.py:23
  372.7 6.7 collective-permute-start.26
  410.1 7.1 collective-permute-start.30
  447.6 7.2 collective-permute-start.34
  449.1 6.9 collective-permute-start.35
  497.6 48.5 %all-to-all-start.2 = ((f32[32,8,512]{2,1,0:T(8,128)}), f32[32,8,512]{2,1,0:T(8,128)}, u32[]{:S(2)}, u32[]{:S(2)}) async-start(f32[32,8,512]{2,1,0:T(8,128)} %reshape_reshape.10), calls=%async_computation.2 | async-start | bytes 1048576 | tf_op jit(solution)/shard_map/all_to_all | solution.py:64
  695.9 7.2 collective-permute-start.46
  697.4 6.9 collective-permute-start.47
  719.3 46.4 %collective-permute-start.48 = (f32[32,1,128]{2,0,1:T(8,128)S(1)}, f32[32,1,128]{2,0,1:T(8,128)S(1)}, u32[]{:S(2)}, u32[]{:S(2)}) collective-permute-start(f32[32,1,128]{2,0,1:T(8,128)S(1)} %copy.539), channel_id=1, source_target_pairs={{1,0},{2,1},{3,2},{4,3},{5,4},{6,5},{7,6},{0,7},{9,8},{10,9},{11,1... | collective-permute-start | bytes 49160 | tf_op jit(solution)/shard_map/ppermute | solution.py:24
  722.6 46.0 %collective-permute-start.49 = (f32[32,1,128]{2,0,1:T(8,128)S(1)}, f32[32,1,128]{2,0,1:T(8,128)S(1)}, u32[]{:S(2)}, u32[]{:S(2)}) collective-permute-start(f32[32,1,128]{2,0,1:T(8,128)S(1)} %copy.541), channel_id=1, source_target_pairs={{0,1},{1,2},{2,3},{3,4},{4,5},{5,6},{6,7},{7,0},{8,9},{9,10},{10,1... | collective-permute-start | bytes 49160 | tf_op jit(solution)/shard_map/ppermute | solution.py:23
  772.5 8.3 collective-permute-start.50
  (91 other events, 662.7 us)

commit v2 on v0

v2 whole, which is shorter than its diff:
```python
import functools

import jax
import jax.numpy as jnp
from jax import lax
from jax.experimental import pallas as pl
from jax.experimental.pallas import tpu as pltpu
from jax.sharding import PartitionSpec as P

FOOT = 4
STEPS = 4
DIFFUSION = 0.15
CENTRE = 1.0 - 4.0 * DIFFUSION
PRECISE = lax.Precision.HIGHEST
MESH = pl.DeviceIdType.MESH
LANES = 128
DEPTH = 8
HLON = 8
HROW = 2
LIMIT = 48 * 1024 * 1024


def place():
    lat_n, lon_n = lax.axis_size("lat"), lax.axis_size("lon")
    lat_i, lon_i = lax.axis_index("lat"), lax.axis_index("lon")
    return lat_n, lon_n, lat_i, lon_i


def greet_all():
    lat_n, lon_n, lat_i, lon_i = place()
    total = lat_n * lon_n
    me = lat_i * lon_n + lon_i
    barrier = pltpu.get_barrier_semaphore()

    def greet(d, carry):
        peer = lax.rem(me + d, total)
        pl.semaphore_signal(
            barrier, inc=1, device_id=(lax.div(peer, lon_n), lax.rem(peer, lon_n)), device_id_type=MESH
        )
        return carry

    lax.fori_loop(1, total, greet, 0)
    pl.semaphore_wait(barrier, total - 1)


def greet_near():
    lat_n, lon_n, lat_i, lon_i = place()
    barrier = pltpu.get_barrier_semaphore()
    for near in (lax.rem(lon_i + 1, lon_n), lax.rem(lon_i + lon_n - 1, lon_n)):
        pl.semaphore_signal(barrier, inc=1, device_id=(lat_i, near), device_id_type=MESH)

    @pl.when(lat_i > 0)
    def _():
        pl.semaphore_signal(barrier, inc=1, device_id=(lat_i - 1, lon_i), device_id_type=MESH)

    @pl.when(lat_i < lat_n - 1)
    def _():
        pl.semaphore_signal(barrier, inc=1, device_id=(lat_i + 1, lon_i), device_id_type=MESH)

    peers = 2 + jnp.where(lat_i > 0, 1, 0) + jnp.where(lat_i < lat_n - 1, 1, 0)
    pl.semaphore_wait(barrier, peers)


def trade_copy(sent, got, send_sems, recv_sems, peer, slot, lon_n):
    return pltpu.make_async_remote_copy(
        src_ref=sent.at[peer],
        dst_ref=got.at[slot],
        send_sem=send_sems.at[peer],
        recv_sem=recv_sems.at[slot],
        device_id=(lax.div(peer, lon_n), lax.rem(peer, lon_n)),
        device_id_type=MESH,
    )


def trade_start(sent, got, send_sems, recv_sems):
    lat_n, lon_n, lat_i, lon_i = place()
    total = lat_n * lon_n
    me = lat_i * lon_n + lon_i

    def send(d, carry):
        peer = lax.rem(me + d, total)
        trade_copy(sent, got, send_sems, recv_sems, peer, me, lon_n).start()
        return carry

    lax.fori_loop(1, total, send, 0)
    got[me] = sent[me]


def trade_wait(sent, got, send_sems, recv_sems):
    lat_n, lon_n, lat_i, lon_i = place()
    total = lat_n * lon_n
    me = lat_i * lon_n + lon_i

    def finish(d, carry):
        peer = lax.rem(me + d, total)
        copy = trade_copy(sent, got, send_sems, recv_sems, peer, peer, lon_n)
        copy.wait_send()
        copy.wait_recv()
        return carry

    lax.fori_loop(1, total, finish, 0)


def part(ref, rows, columns):
    if len(ref.shape) == 4:
        return ref.at[:, pl.ds(*rows), pl.ds(*columns)]
    return ref.at[pl.ds(*rows), pl.ds(*columns)]


def halo_copies(wide, send_sems, recv_sems):
    lat_n, lon_n, lat_i, lon_i = place()
    rows, columns = wide.shape[-3], wide.shape[-2]
    inner = (HLON, columns - 2 * HLON)

    def copy(index, source, target, device):
        return pltpu.make_async_remote_copy(
            src_ref=source,
            dst_ref=target,
            send_sem=send_sems.at[index],
            recv_sem=recv_sems.at[index],
            device_id=device,
            device_id_type=MESH,
        )

    down = copy(0, part(wide, (HROW, HROW), inner), part(wide, (rows - HROW, HROW), inner), (lat_i - 1, lon_i))
    up = copy(1, part(wide, (rows - 2 * HROW, HROW), inner), part(wide, (0, HROW), inner), (lat_i + 1, lon_i))
    west = copy(
        2,
        part(wide, (0, rows), (HLON, HLON)),
        part(wide, (0, rows), (columns - HLON, HLON)),
        (lat_i, lax.rem(lon_i + lon_n - 1, lon_n)),
    )
    east = copy(
        3,
        part(wide, (0, rows), (columns - 2 * HLON, HLON)),
        part(wide, (0, rows), (0, HLON)),
        (lat_i, lax.rem(lon_i + 1, lon_n)),
    )
    return down, up, west, east


def lat_edges(wide):
    lat_n, lon_n, lat_i, lon_i = place()
    rows = wide.shape[-3]
    for ends, first in ((lat_i == 0, 0), (lat_i == lat_n - 1, rows - HROW)):

        @pl.when(ends)
        def _(first=first):
            if len(wide.shape) == 4:
                for index in range(wide.shape[0]):
                    for row in range(HROW):
                        wide[index, first + row] = jnp.zeros(wide.shape[2:], jnp.float32)
            else:
                for row in range(HROW):
                    wide[first + row] = jnp.zeros(wide.shape[1:], jnp.float32)


def lat_start(down, up):
    lat_n, lon_n, lat_i, lon_i = place()

    @pl.when(lat_i > 0)
    def _():
        down.start()

    @pl.when(lat_i < lat_n - 1)
    def _():
        up.start()


def lat_wait(down, up):
    lat_n, lon_n, lat_i, lon_i = place()

    @pl.when(lat_i > 0)
    def _():
        down.wait_send()
        up.wait_recv()

    @pl.when(lat_i < lat_n - 1)
    def _():
        up.wait_send()
        down.wait_recv()


def dot(left, right, axes=((1,), (0,))):
    return lax.dot_general(
        left, right, (axes, ((), ())), precision=PRECISE, preferred_element_type=jnp.float32
    )


def full_sum(values):
    return jnp.sum(jnp.sum(values, axis=0, keepdims=True), axis=1, keepdims=True)


def gathered_sum(got, first, lane_index):
    tile = jnp.sum(got[:, :, first : first + LANES], axis=0)
    lane = lax.broadcasted_iota(jnp.int32, tile.shape, 1)
    row = lax.broadcasted_iota(jnp.int32, tile.shape, 0)
    return full_sum(jnp.where((lane == lane_index) & (row == 0), tile, 0.0))


def first_kernel(
    count, owner, spot, innovations, matrix, fields,
    rows_out, anchors_out, permuted, residual, packing, norm_out, wide,
    sent, got, send_sems, recv_sems, halo_send, halo_recv,
):
    slots, block_total = packing.shape
    total = slots // DEPTH
    width = matrix.shape[0]
    field_rows, field_columns = fields.shape[1], fields.shape[2]

    def fill(row, carry):
        for index in range(3):
            wide[index, HROW + row, pl.ds(HLON, field_columns)] = fields[index, row]
        return carry

    lax.fori_loop(0, field_rows, fill, 0)
    lat_edges(wide)
    down, up, west, east = halo_copies(wide, halo_send, halo_recv)
    greet_all()
    lat_start(down, up)

    live_column = lax.broadcasted_iota(jnp.int32, (block_total, 1), 0) < count[0]
    start = jnp.where(live_column, dot(innovations[...], matrix[...], ((1,), (1,))), 0.0)
    residual[...] = start
    row = lax.broadcasted_iota(jnp.int32, (width, width), 0)
    column = lax.broadcasted_iota(jnp.int32, (width, width), 1)
    footprint = FOOT * FOOT
    shuffle = column == lax.rem(row, footprint) * (width // footprint) + lax.div(row, footprint)
    permuted[...] = dot(matrix[...], shuffle.astype(jnp.float32))
    weighted = dot(start, permuted[...])

    live_row = lax.broadcasted_iota(jnp.int32, (1, block_total), 1) < count[0]
    owners = owner[...]
    tiles = lax.broadcasted_iota(jnp.int32, (total, block_total), 0)
    named = jnp.where((tiles == owners) & live_row, 1.0, 0.0)
    earlier = lax.broadcasted_iota(jnp.int32, (block_total, block_total), 0) < lax.broadcasted_iota(
        jnp.int32, (block_total, block_total), 1
    )
    ranks = jnp.sum(named * dot(named, earlier.astype(jnp.float32)), axis=0, keepdims=True)
    target = owners.astype(jnp.float32) * DEPTH + ranks
    slot_ids = lax.broadcasted_iota(jnp.int32, (slots, block_total), 0).astype(jnp.float32)
    pack = jnp.where((slot_ids == target) & live_row, 1.0, 0.0)
    packing[...] = pack
    sent[:, :, :width] = dot(pack, weighted).reshape(total, DEPTH, width)
    lane = lax.broadcasted_iota(jnp.int32, (slots, LANES), 1)
    spots = jnp.where(lane == 2, full_sum(start * start), dot(pack, spot[...]))
    sent[:, :, width:] = spots.reshape(total, DEPTH, LANES)
    trade_start(sent, got, send_sems, recv_sems)
    lat_wait(down, up)
    west.start()
    east.start()
    trade_wait(sent, got, send_sems, recv_sems)
    unload(got, rows_out)
    anchors_out[...] = got[:, :, width:].reshape(slots, LANES)
    norm_out[...] = jnp.broadcast_to(gathered_sum(got, width, 2), norm_out.shape)
    west.wait()
    east.wait()


def unload(got, rows_out):
    slots, groups = rows_out.shape[:2]
    for group in range(groups):
        rows_out[:, group, :] = got[:, :, group * LANES : (group + 1) * LANES].reshape(slots, LANES)


def spread_kernel(anchors, rows, field):
    slots = rows.shape[0]
    level_lanes = LANES // FOOT
    field[...] = jnp.zeros(field.shape, jnp.float32)

    def add(slot, carry):
        column, latitude = anchors[slot], anchors[slots + slot]
        row, shift = lax.div(latitude, FOOT), lax.rem(latitude, FOOT) * level_lanes
        patch = pltpu.roll(rows[slot], shift, 1)
        lane = lax.broadcasted_iota(jnp.int32, patch.shape, 1)
        here = lane >= shift
        field[row, pl.ds(column, FOOT), :] += jnp.where(here, patch, 0.0)
        field[row + 1, pl.ds(column, FOOT), :] += jnp.where(here, 0.0, patch)
        return carry

    lax.fori_loop(0, slots, add, 0, unroll=4)


def sample_kernel(anchors, field, rows):
    slots = rows.shape[0]
    level_lanes = LANES // FOOT

    def pick(slot, carry):
        column, latitude = anchors[slot], anchors[slots + slot]
        row, shift = lax.div(latitude, FOOT), lax.rem(latitude, FOOT) * level_lanes
        here = field[row, pl.ds(column, FOOT), :]
        after = field[row + 1, pl.ds(column, FOOT), :]
        lane = lax.broadcasted_iota(jnp.int32, here.shape, 1)
        rows[slot] = pltpu.roll(jnp.where(lane >= shift, here, after), lax.rem(LANES - shift, LANES), 1)
        return carry

    lax.fori_loop(0, slots, pick, 0, unroll=8)


def model_step(now, later, wide, adjoint):
    lat_n, lon_n, lat_i, lon_i = place()
    rows, columns = now.shape[0], now.shape[1]
    level_lanes = LANES // FOOT
    low = jnp.where(lat_i > 0, 1.0, 0.0)
    high = jnp.where(lat_i < lat_n - 1, 1.0, 0.0)
    lane = lax.broadcasted_iota(jnp.int32, (columns, LANES), 1)
    first, last = lane < level_lanes, lane >= LANES - level_lanes

    def plane(row, carry):
        before, after = lax.rem(row + rows - 1, rows), lax.rem(row + 1, rows)
        here = now[row]
        prior = jnp.where(last, now[before], here)
        following = jnp.where(first, now[after], here)
        zonal, meridional = 0.5 * wide[0, row], wide[1, row]
        if adjoint:
            prior_wind = jnp.where(last, wide[1, before], meridional)
            next_wind = jnp.where(first, wide[1, after], meridional)
            value = (
                CENTRE * here
                + pltpu.roll((DIFFUSION - zonal) * here, 1, 0)
                + pltpu.roll((DIFFUSION + zonal) * here, columns - 1, 0)
                + pltpu.roll((DIFFUSION - 0.5 * prior_wind) * prior, level_lanes, 1)
                + pltpu.roll((DIFFUSION + 0.5 * next_wind) * following, LANES - level_lanes, 1)
            )
        else:
            value = (
                CENTRE * here
                + (DIFFUSION - zonal) * pltpu.roll(here, columns - 1, 0)
                + (DIFFUSION + zonal) * pltpu.roll(here, 1, 0)
                + (DIFFUSION - 0.5 * meridional) * pltpu.roll(following, LANES - level_lanes, 1)
                + (DIFFUSION + 0.5 * meridional) * pltpu.roll(prior, level_lanes, 1)
            )
        keep = jnp.where(row < HROW, low, jnp.where(row >= rows - HROW, high, 1.0))
        later[row] = value * keep
        return carry

    lax.fori_loop(0, rows, plane, 0)


def model_steps(held, other, wide, adjoint):
    def pair(index, carry):
        model_step(held, other, wide, adjoint)
        model_step(other, held, wide, adjoint)
        return carry

    lax.fori_loop(0, STEPS // 2, pair, 0)


def load_wide(field, held, send_sems, recv_sems, greet):
    columns = field.shape[1]

    def fill(row, carry):
        held[HROW + row, pl.ds(HLON, columns)] = field[row]
        return carry

    lax.fori_loop(0, held.shape[0] - 2 * HROW, fill, 0)
    lat_edges(held)
    down, up, west, east = halo_copies(held, send_sems, recv_sems)
    greet()
    lat_start(down, up)
    lat_wait(down, up)
    west.start()
    east.start()
    west.wait()
    east.wait()


def system_kernel(field, wide, adjoint_out, forward_out, energy_out, held, other, send_sems, recv_sems):
    rows, columns = held.shape[0], held.shape[1]
    own = columns - 2 * HLON
    load_wide(field, held, send_sems, recv_sems, greet_near)
    model_steps(held, other, wide, True)

    def scale(row, energy):
        value, deviation = held[row], wide[2, row]
        scaled = deviation * deviation * value
        held[row] = scaled
        adjoint_out[row - HROW] = value[HLON : HLON + own]
        return energy + (scaled * value)[HLON : HLON + own]

    energy = lax.fori_loop(HROW, rows - HROW, scale, jnp.zeros((own, LANES), jnp.float32))
    energy_out[...] = jnp.broadcast_to(full_sum(energy), energy_out.shape)
    for row in (*range(HROW), *range(rows - HROW, rows)):
        deviation = wide[2, row]
        held[row] = deviation * deviation * held[row]
    model_steps(held, other, wide, False)

    def write(row, carry):
        forward_out[row] = held[HROW + row, pl.ds(HLON, own)]
        return carry

    lax.fori_loop(0, rows - 2 * HROW, write, 0)
    forward_out[rows - 2 * HROW] = jnp.zeros((own, LANES), jnp.float32)


def return_kernel(
    rows, energy, matrix, start, packing, norm,
    rows_out, direction, step_out, ratio_out, norm_out, square_out,
    sent, got, sent_next, got_next, send_sems, recv_sems, send_next, recv_next,
):
    slots, groups = rows.shape[:2]
    total = slots // DEPTH
    width = matrix.shape[0]
    for group in range(groups):
        sent[:, :, group * LANES : (group + 1) * LANES] = rows[:, group, :].reshape(total, DEPTH, LANES)
    sent[:, :, width:] = jnp.broadcast_to(energy[...][None], (total, DEPTH, LANES))
    greet_all()
    trade_start(sent, got, send_sems, recv_sems)
    trade_wait(sent, got, send_sems, recv_sems)
    norm_first = norm[0:1, 0:1]
    step = norm_first / (norm_first + gathered_sum(got, width, 0))
    back = dot(packing[...], got[:, :, :width].reshape(slots, width), ((0,), (0,)))
    image = start[...] + dot(back, matrix[...], ((1,), (1,)))
    residual = start[...] - step * image
    pack = packing[...]
    sent_next[:, :, :width] = dot(pack, dot(residual, matrix[...])).reshape(total, DEPTH, width)
    sent_next[:, :, width:] = jnp.broadcast_to(full_sum(residual * residual)[None], (total, DEPTH, LANES))
    trade_start(sent_next, got_next, send_next, recv_next)
    trade_wait(sent_next, got_next, send_next, recv_next)
    unload(got_next, rows_out)
    norm_next = gathered_sum(got_next, width, 0)
    ratio = norm_next / norm_first
    moved = residual + ratio * start[...]
    direction[...] = moved
    step_out[...] = jnp.broadcast_to(step, step_out.shape)
    ratio_out[...] = jnp.broadcast_to(ratio, ratio_out.shape)
    norm_out[...] = jnp.broadcast_to(norm_next, norm_out.shape)
    square_out[...] = jnp.broadcast_to(full_sum(moved * moved), square_out.shape)


def last_kernel(
    field, wide, earlier, ratio, norm, square,
    adjoint_out, step_out,
    held, other, sent, got, halo_send, halo_recv, send_sems, recv_sems,
):
    rows, columns = held.shape[0], held.shape[1]
    own = columns - 2 * HLON
    load_wide(field, held, halo_send, halo_recv, greet_all)
    model_steps(held, other, wide, True)
    scale = ratio[0:1, 0:1]

    def combine(row, energy):
        value = held[HROW + row, pl.ds(HLON, own)] + scale * earlier[row]
        adjoint_out[row] = value
        deviation = wide[2, HROW + row, pl.ds(HLON, own)] * value
        return energy + deviation * deviation

    energy = lax.fori_loop(0, rows - 2 * HROW, combine, jnp.zeros((own, LANES), jnp.float32))
    sent[...] = jnp.broadcast_to((full_sum(energy) + square[0:1, 0:1])[None], sent.shape)
    trade_start(sent, got, send_sems, recv_sems)
    trade_wait(sent, got, send_sems, recv_sems)
    step_out[...] = jnp.broadcast_to(norm[0:1, 0:1] / gathered_sum(got, 0, 0), step_out.shape)


def vmem(count):
    return [pl.BlockSpec(memory_space=pltpu.VMEM)] * count


def smem():
    return pl.BlockSpec(memory_space=pltpu.SMEM)


def shape(*sizes):
    return jax.ShapeDtypeStruct(sizes, jnp.float32)


def params(collective_id=None):
    if collective_id is None:
        return pltpu.CompilerParams(vmem_limit_bytes=LIMIT)
    return pltpu.CompilerParams(
        collective_id=collective_id, has_side_effects=True, vmem_limit_bytes=LIMIT
    )


def folded(values):
    levels, columns, latitudes = values.shape
    return (
        values.reshape(levels, columns, latitudes // FOOT, FOOT)
        .transpose(2, 1, 3, 0)
        .reshape(latitudes // FOOT, columns, FOOT * levels)
    )


def unfolded(values, levels):
    rows, columns, _ = values.shape
    return values.reshape(rows, columns, FOOT, levels).transpose(3, 1, 0, 2).reshape(levels, columns, rows * FOOT)


def body(
    innovations, block_owner, block_lat, block_lon, block_count,
    error_weight, courant_lon, courant_lat, background_std,
):
    total = lax.axis_size("lat") * lax.axis_size("lon")
    block_total, width = innovations.shape
    levels, columns, latitudes = courant_lon.shape
    rows = latitudes // FOOT
    slots = total * DEPTH
    groups = width // LANES
    wide_rows, wide_columns = rows + 2 * HROW, columns + 2 * HLON
    fields = jnp.stack([folded(courant_lon), folded(courant_lat), folded(background_std)])
    spot = jnp.pad(
        jnp.stack([block_lon, block_lat], axis=1).astype(jnp.float32), ((0, 0), (0, LANES - 2))
    )
    tile = shape(DEPTH, LANES)
    chunks = pltpu.VMEM((total, DEPTH, width + LANES), jnp.float32)
    dma = pltpu.SemaphoreType.DMA

    arrived, anchors, matrix, start, packing, norm, wide = pl.pallas_call(
        first_kernel,
        out_shape=(
            shape(slots, groups, LANES), shape(slots, LANES), shape(width, width),
            shape(block_total, width), shape(slots, block_total), tile,
            shape(3, wide_rows, wide_columns, LANES),
        ),
        in_specs=[smem()] + vmem(5),
        out_specs=tuple(vmem(7)),
        scratch_shapes=[chunks, chunks, dma((total,)), dma((total,)), dma((4,)), dma((4,))],
        compiler_params=params(0),
    )(block_count, block_owner.reshape(1, block_total), spot, innovations, error_weight[0], fields)

    corners = jnp.concatenate([anchors[:, 0], anchors[:, 1]]).astype(jnp.int32)

    def spread(block_rows):
        return pl.pallas_call(
            spread_kernel,
            out_shape=shape(rows + 1, columns, LANES),
            in_specs=[smem()] + vmem(1),
            out_specs=vmem(1)[0],
            compiler_params=params(),
        )(corners, block_rows)

    held = pltpu.VMEM((wide_rows, wide_columns, LANES), jnp.float32)
    first, model_state, energy = pl.pallas_call(
        system_kernel,
        out_shape=(shape(rows, columns, LANES), shape(rows + 1, columns, LANES), tile),
        in_specs=vmem(2),
        out_specs=tuple(vmem(3)),
        scratch_shapes=[held, held, dma((4,)), dma((4,))],
        compiler_params=params(1),
    )(spread(arrived), wide)

    picked = pl.pallas_call(
        sample_kernel,
        out_shape=shape(slots, groups, LANES),
        in_specs=[smem()] + vmem(1),
        out_specs=vmem(1)[0],
        compiler_params=params(),
    )(corners, model_state)

    arrived, direction, step_first, ratio, norm_next, square = pl.pallas_call(
        return_kernel,
        out_shape=(shape(slots, groups, LANES), shape(block_total, width), tile, tile, tile, tile),
        in_specs=vmem(6),
        out_specs=tuple(vmem(6)),
        scratch_shapes=[chunks, chunks, chunks, chunks] + [dma((total,))] * 4,
        compiler_params=params(2),
    )(picked, energy, matrix, start, packing, norm)

    tiles = pltpu.VMEM((total, DEPTH, LANES), jnp.float32)
    second, step_second = pl.pallas_call(
        last_kernel,
        out_shape=(shape(rows, columns, LANES), tile),
        in_specs=vmem(6),
        out_specs=tuple(vmem(2)),
        scratch_shapes=[held, held, tiles, tiles, dma((4,)), dma((4,)), dma((total,)), dma((total,))],
        compiler_params=params(3),
    )(spread(arrived), wide, first, ratio, norm_next, square)

    step_first, step_second = step_first[0, 0], step_second[0, 0]
    solution = step_first * start + step_second * direction
    increment = unfolded(step_first * first + step_second * second, levels)
    return solution, background_std * background_std * increment


def solution(mesh):
    blocks = P(("lat", "lon"))
    in_specs = (
        P(("lat", "lon"), None),
        P(("lat", "lon"), None),
        blocks,
        blocks,
        blocks,
        P(("lat", "lon"), None, None),
        P(None, "lon", "lat"),
        P(None, "lon", "lat"),
        P(None, "lon", "lat"),
    )
    out_specs = (P(("lat", "lon"), None), P(None, "lon", "lat"))
    return jax.shard_map(body, mesh=mesh, in_specs=in_specs, out_specs=out_specs, check_vma=False)
```

time: 1250 us -> 203 us (0.16)
  local copies, waits for them, and re-layouts: 438 us -> 29.3 us
  other arithmetic: 337 us -> 8.69 us
  starting transfers between devices: 184 us -> 0 us
  blocking collectives: 181 us -> 0 us
  Pallas kernels: 0 us -> 163 us
  waiting for transfers between devices: 81 us -> 0 us
    add x20 -> x2, other arithmetic: 185 us -> 3.26 us  [the longest x1 1.97 us: body(): solution = step_first * start + step_second * direction]
    ppermute x84 -> x0, starting transfers between devices: 170 us -> none  [the longest x42 112 us: with_halo(): before = lax.ppermute(last, axis, up)]
    pallas_call x0 -> x7, Pallas kernels: none -> 163 us  [the longest x1 40.4 us: body(): pl.pallas_call(return_kernel, out_shape=(shape(slots, groups, LANES), sha...]
    slice x61 -> x3, local copies, waits for them, and re-layouts: 161 us -> 1.23 us  [the longest x2 1.03 us: body(): step_first, step_second = (step_first[0, 0], step_second[0, 0])]
    ppermute x42 -> x0, local copies, waits for them, and re-layouts: 121 us -> none  [the longest x21 61 us: with_halo(): before = lax.ppermute(last, axis, up)]
    psum x3 -> x0, blocking collectives: 116 us -> none  [the longest x2 78.9 us: squares(): return lax.psum(jnp.sum(residual * residual), ('lat', 'lon'))]
    scatter-add x3 -> x0, other arithmetic: 72.8 us -> none  [spread_rows(): flat_field = jnp.zeros((LEV, field_shape[1] * field_shape[2]), jnp.float3...]
    all_to_all x3 -> x0, blocking collectives: 64.2 us -> none  [trade_blocks(): lax.all_to_all(direct, ('lat', 'lon'), split_axis=0, concat_axis=0, tiled...]
  transfers between devices with their start and end apart: 87 -> 0, of which waited for: 39 -> 0; matrix products, arithmetic and copies ran while one was open for 17% -> 0% of each run, Pallas kernels for 0% -> 0%
where the time goes in v2:
time: 203 us; the launch traced here: 202 us
  Pallas kernels  163 us (80%)
  local copies, waits for them, and re-layouts  29.3 us (14%)
  other arithmetic  8.69 us (4%)
    pallas_call x1, Pallas kernels, body(): pl.pallas_call(return_kernel, out_shape=(shape(slots, groups, LANES), sha...  40.4 us
    pallas_call x1, Pallas kernels, body(): pl.pallas_call(system_kernel, out_shape=(shape(rows, columns, LANES), sha...  38.7 us
    pallas_call x1, Pallas kernels, body(): pl.pallas_call(first_kernel, out_shape=(shape(slots, groups, LANES), shap...  35.1 us
    pallas_call x1, Pallas kernels, body(): pl.pallas_call(last_kernel, out_shape=(shape(rows, columns, LANES), tile)...  32.7 us
    unnamed x16, local copies, waits for them, and re-layouts  15.3 us
    pallas_call x2, Pallas kernels, spread(): pl.pallas_call(spread_kernel, out_shape=shape(rows + 1, columns, LANES),...  12.4 us
    another operation x3, local copies, waits for them, and re-layouts, body(): jnp.stack([folded(courant_lon), folded(courant_lat), folded(background_st...  5.75 us
    transpose x1, local copies, waits for them, and re-layouts, unfolded(): values.reshape(rows, columns, FOOT, levels).transpose(3, 1, 0, 2)  4.28 us

profile of v2, /device:TPU:0, one launch (start us, length us, event | category | flops | bytes accessed | tf_op | source)
XLA Modules:
  0.0 202.3 jit_solution(4248977472354721148)
XLA Ops:
  1.3 0.7 add_convert_fusion
  2.1 3.0 %copy.45 = f32[32,40,128]{1,0,2:T(8,128)S(1)} copy(f32[32,40,128]{2,1,0:T(8,128)} %param.17) | data formatting | bytes 1310720 | tf_op args[8]
  5.1 0.6 copy.53
  5.7 2.8 %copy.41 = f32[32,40,128]{1,0,2:T(8,128)} copy(f32[32,40,128]{2,1,0:T(8,128)S(1)} %copy-done.5) | data formatting | bytes 1310720 | tf_op args[6]
  8.5 2.2 %copy.51 = f32[1,32,40,128]{3,2,1,0:T(8,128)S(1)} copy(f32[1,32,40,128]{2,3,1,0:T(8,128)} %bitcast.28) | data formatting | bytes 1310720 | tf_op jit(solution)/shard_map/stack;reshape | solution.py:500
  10.7 3.9 %copy.43 = f32[32,40,128]{1,0,2:T(8,128)} copy(f32[32,40,128]{2,1,0:T(8,128)} %param.16) | data formatting | bytes 1310720 | tf_op args[7]
  14.6 3.0 %copy.52 = f32[1,32,40,128]{3,2,1,0:T(8,128)} copy(f32[1,32,40,128]{2,3,1,0:T(8,128)} %bitcast.29) | data formatting | bytes 1310720 | tf_op jit(solution)/shard_map/stack;reshape | solution.py:500
  17.6 1.3 pad_maximum_fusion.fields
  19.1 35.1 %shard_map.104 = (f32[256,4,128]{2,1,0:T(4,128)S(1)}, f32[256,128]{1,0:T(8,128)S(1)}, f32[512,512]{1,0:T(8,128)S(1)}, f32[128,512]{1,0:T(8,128)S(1)}, f32[256,12...) custom-call(s32[1]{0:T(128)S(6)} %copy.54.count, s32[1,128]{1,0:T(1,128)S(1)} %bitcast.25, ...), custom_call_target="tpu_custom_call" | custom-call | tf_op jit(solution)/shard_map/pallas_call | solution.py:508
  54.4 6.2 %shard_map.105.field = f32[33,40,128]{2,1,0:T(8,128)S(1)} custom-call(s32[512]{0:T(512)S(1)} %maximum_convert_fusion.anchors, f32[256,4,128]{2,1,0:T(4,128)S(1)} %get-tuple-element.21.rows), custom_call_target="tpu_custom_call" | custom-call | tf_op jit(solution)/shard_map/pallas_call | solution.py:524
  60.6 1.9 copy-done
  62.5 38.7 %shard_map.106 = (f32[32,40,128]{2,1,0:T(8,128)S(1)}, f32[33,40,128]{2,1,0:T(8,128)S(1)}, f32[8,128]{1,0:T(8,128)S(1)}) custom-call(f32[33,40,128]{2,1,0:T(8,128)S(1)} %shard_map.105.field, f32[3,36,56,128]{3,2,1,0:T(8,128)S(1)} %copy-done), custom_call_target="tpu_custom_call" | custom-call | tf_op jit(solution)/shard_map/pallas_call | solution.py:533
  101.2 3.8 %shard_map.107.rows = f32[256,4,128]{2,1,0:T(4,128)S(1)} custom-call(s32[512]{0:T(512)S(1)} %maximum_convert_fusion.anchors, f32[33,40,128]{2,1,0:T(8,128)S(1)} %get-tuple-element.23.field), custom_call_target="tpu_custom_call" | custom-call | tf_op jit(solution)/shard_map/pallas_call | solution.py:542
  104.9 40.4 %shard_map.108 = (f32[256,4,128]{2,1,0:T(4,128)S(1)}, f32[128,512]{1,0:T(8,128)S(1)}, f32[8,128]{1,0:T(8,128)S(1)}, f32[8,128]{1,0:T(8,128)S(1)}, f32[8,128]{1,0:T(8,128)S(1)}, /*index=5*/f32[8,128]{1,0:T(8,128)S(1)}) custom-call(f32[256,4,128]{2,1,0:T(4,128)S(1)} %shard_map.107.rows, f32[8,128]{1,0:T(8,128)S(1)} %get-tuple-element.24.energy, ...), custom_call_target="tpu_custom_call" | custom-call | tf_op jit(solution)/shard_map/pallas_call | solution.py:550
  145.3 0.5 slice.14
  145.8 6.2 %shard_map.109.field = f32[33,40,128]{2,1,0:T(8,128)S(1)} custom-call(s32[512]{0:T(512)S(1)} %maximum_convert_fusion.anchors, f32[256,4,128]{2,1,0:T(4,128)S(1)} %get-tuple-element.30.rows), custom_call_target="tpu_custom_call" | custom-call | tf_op jit(solution)/shard_map/pallas_call | solution.py:524
  152.0 32.7 %shard_map.110 = (f32[32,40,128]{2,1,0:T(8,128)S(1)}, f32[8,128]{1,0:T(8,128)S(1)}) custom-call(f32[33,40,128]{2,1,0:T(8,128)S(1)} %shard_map.109.field, f32[3,36,56,128]{3,2,1,0:T(8,128)S(1)} %copy-done.1, f32[32,40,128]{2,1,0:T(8,128)S(1)} %get-tuple-element.31.earlier, f32[8,128]{1,0:T(8,128)S(1)} %get-tuple-element.32.ratio, ...), custom_call_target="tpu_custom_call" | custom-call | tf_op jit(solution)/shard_map/pallas_call | solution.py:560
  184.7 0.5 slice.15
  185.2 1.3 multiply_add_fusion
  186.5 2.0 multiply_add_fusion.1
  188.5 2.6 %reshape.26 = f32[32,40,4,32]{3,2,1,0:T(4,128)} reshape(f32[32,40,128]{2,1,0:T(8,128)S(1)} %multiply_add_fusion) | data formatting | bytes 1310720 | tf_op jit(solution)/shard_map/reshape | solution.py:486
  191.1 4.3 %copy.49 = f32[32,40,32,4]{1,0,3,2:T(8,128)} copy(f32[32,40,32,4]{0,3,1,2:T(4,128)} %bitcast.27) | data formatting | bytes 1310720 | tf_op jit(solution)/shard_map/transpose | solution.py:486
  195.4 3.4 %bitcast_multiply_fusion = f32[32,40,128]{1,0,2:T(8,128)} fusion(f32[32,40,32,4]{1,0,3,2:T(8,128)} %copy.49, f32[32,40,128]{1,0,2:T(8,128)S(1)} %copy.45), kind=kLoop, calls=%fused_computation | loop fusion | flops 327680 | bytes 1966080 | tf_op jit(solution)/shard_map/mul | solution.py:572
  198.8 3.5 %copy.50 = f32[32,40,128]{2,1,0:T(8,128)} copy(f32[32,40,128]{1,0,2:T(8,128)} %bitcast_multiply_fusion) | data formatting | bytes 1310720
  (15 shorter events, 0.5 us)
Async XLA Ops:
  2.1 3.6 %copy-start.5 = (f32[32,40,128]{2,1,0:T(8,128)S(1)}, f32[32,40,128]{2,1,0:T(8,128)}, u32[]{:S(2)}) copy-start(f32[32,40,128]{2,1,0:T(8,128)} %param.15) | copy-start | bytes 1966084
  17.6 1.4 copy-start.2
  17.6 1.5 copy-start.3
  17.6 1.5 copy-start.4
  60.6 1.9 copy-start
  101.1 50.9 %copy-start.1 = (f32[3,36,56,128]{3,2,1,0:T(8,128)S(1)}, f32[3,36,56,128]{3,2,1,0:T(8,128)}, u32[]{:S(2)}) copy-start(f32[3,36,56,128]{3,2,1,0:T(8,128)} %get-tuple-element.22.wide) | copy-start | bytes 9289732

commit v3 on v2

--- a/solution.py
+++ b/solution.py
@@ -26,7 +26,7 @@
     return lat_n, lon_n, lat_i, lon_i
 
 
-def greet_all():
+def signal_all():
     lat_n, lon_n, lat_i, lon_i = place()
     total = lat_n * lon_n
     me = lat_i * lon_n + lon_i
@@ -40,10 +40,14 @@
         return carry
 
     lax.fori_loop(1, total, greet, 0)
-    pl.semaphore_wait(barrier, total - 1)
-
-
-def greet_near():
+
+
+def wait_all():
+    lat_n, lon_n, lat_i, lon_i = place()
+    pl.semaphore_wait(pltpu.get_barrier_semaphore(), lat_n * lon_n - 1)
+
+
+def signal_near():
     lat_n, lon_n, lat_i, lon_i = place()
     barrier = pltpu.get_barrier_semaphore()
     for near in (lax.rem(lon_i + 1, lon_n), lax.rem(lon_i + lon_n - 1, lon_n)):
@@ -57,8 +61,11 @@
     def _():
         pl.semaphore_signal(barrier, inc=1, device_id=(lat_i + 1, lon_i), device_id_type=MESH)
 
+
+def wait_near():
+    lat_n, lon_n, lat_i, lon_i = place()
     peers = 2 + jnp.where(lat_i > 0, 1, 0) + jnp.where(lat_i < lat_n - 1, 1, 0)
-    pl.semaphore_wait(barrier, peers)
+    pl.semaphore_wait(pltpu.get_barrier_semaphore(), peers)
 
 
 def trade_copy(sent, got, send_sems, recv_sems, peer, slot, lon_n):
@@ -198,27 +205,67 @@
     return full_sum(jnp.where((lane == lane_index) & (row == 0), tile, 0.0))
 
 
+def chooser(latitudes):
+    rows = latitudes // FOOT
+    row = lax.broadcasted_iota(jnp.int32, (latitudes, latitudes), 0)
+    column = lax.broadcasted_iota(jnp.int32, (latitudes, latitudes), 1)
+    return (column == lax.rem(row, rows) * FOOT + lax.div(row, rows)).astype(jnp.float32)
+
+
+def regroup(pieces, levels):
+    block = lax.div(lax.broadcasted_iota(jnp.int32, pieces[0][0].shape, 1), levels)
+    grouped = []
+    for i in range(FOOT):
+        value = pieces[i][i]
+        for q in range(FOOT):
+            if q != i:
+                moved = pltpu.roll(pieces[q][i], (q - i) % FOOT * levels, 1)
+                value = jnp.where(block == q, moved, value)
+        grouped.append(value)
+    return grouped
+
+
+def fold(natural, store):
+    levels, columns, latitudes = natural.shape
+    rows = latitudes // FOOT
+    choose = chooser(latitudes)
+
+    def group(index, carry):
+        stack = jnp.concatenate([natural[:, FOOT * index + i, :] for i in range(FOOT)], axis=0)
+        mixed = dot(choose, stack, ((1,), (1,)))
+        pieces = [[mixed[q * rows : (q + 1) * rows]] * FOOT for q in range(FOOT)]
+        for i, value in enumerate(regroup(pieces, levels)):
+            store(FOOT * index + i, value)
+        return carry
+
+    lax.fori_loop(0, columns // FOOT, group, 0)
+
+
+def unfold(folded, natural):
+    levels, columns, latitudes = natural.shape
+    choose = chooser(latitudes)
+
+    def group(index, carry):
+        planes = [folded[:, FOOT * index + i, :] for i in range(FOOT)]
+        mixed = jnp.concatenate(regroup([[plane] * FOOT for plane in planes], levels), axis=0)
+        stack = dot(mixed, choose, ((0,), (0,)))
+        for i in range(FOOT):
+            natural[:, FOOT * index + i, :] = stack[i * levels : (i + 1) * levels]
+        return carry
+
+    lax.fori_loop(0, columns // FOOT, group, 0)
+
+
 def first_kernel(
-    count, owner, spot, innovations, matrix, fields,
+    count, owner, spot, innovations, matrix, courant_lon, courant_lat, deviation,
     rows_out, anchors_out, permuted, residual, packing, norm_out, wide,
     sent, got, send_sems, recv_sems, halo_send, halo_recv,
 ):
     slots, block_total = packing.shape
     total = slots // DEPTH
     width = matrix.shape[0]
-    field_rows, field_columns = fields.shape[1], fields.shape[2]
-
-    def fill(row, carry):
-        for index in range(3):
-            wide[index, HROW + row, pl.ds(HLON, field_columns)] = fields[index, row]
-        return carry
-
-    lax.fori_loop(0, field_rows, fill, 0)
     lat_edges(wide)
-    down, up, west, east = halo_copies(wide, halo_send, halo_recv)
-    greet_all()
-    lat_start(down, up)
-
+    signal_all()
     live_column = lax.broadcasted_iota(jnp.int32, (block_total, 1), 0) < count[0]
     start = jnp.where(live_column, dot(innovations[...], matrix[...], ((1,), (1,))), 0.0)
     residual[...] = start
@@ -226,8 +273,8 @@
     column = lax.broadcasted_iota(jnp.int32, (width, width), 1)
     footprint = FOOT * FOOT
     shuffle = column == lax.rem(row, footprint) * (width // footprint) + lax.div(row, footprint)
-    permuted[...] = dot(matrix[...], shuffle.astype(jnp.float32))
-    weighted = dot(start, permuted[...])
+    shuffle = shuffle.astype(jnp.float32)
+    weighted = dot(dot(start, matrix[...]), shuffle)
 
     live_row = lax.broadcasted_iota(jnp.int32, (1, block_total), 1) < count[0]
     owners = owner[...]
@@ -245,7 +292,17 @@
     lane = lax.broadcasted_iota(jnp.int32, (slots, LANES), 1)
     spots = jnp.where(lane == 2, full_sum(start * start), dot(pack, spot[...]))
     sent[:, :, width:] = spots.reshape(total, DEPTH, LANES)
+    wait_all()
     trade_start(sent, got, send_sems, recv_sems)
+    for index, natural in enumerate((courant_lon, courant_lat, deviation)):
+
+        def store(place_in, value, index=index):
+            wide[index, pl.ds(HROW, value.shape[0]), HLON + place_in, :] = value
+
+        fold(natural, store)
+    down, up, west, east = halo_copies(wide, halo_send, halo_recv)
+    lat_start(down, up)
+    permuted[...] = dot(matrix[...], shuffle)
     lat_wait(down, up)
     west.start()
     east.start()
@@ -278,7 +335,7 @@
         field[row + 1, pl.ds(column, FOOT), :] += jnp.where(here, 0.0, patch)
         return carry
 
-    lax.fori_loop(0, slots, add, 0, unroll=4)
+    lax.fori_loop(0, slots, add, 0, unroll=8)
 
 
 def sample_kernel(anchors, field, rows):
@@ -334,7 +391,7 @@
         later[row] = value * keep
         return carry
 
-    lax.fori_loop(0, rows, plane, 0)
+    lax.fori_loop(0, rows, plane, 0, unroll=4)
 
 
 def model_steps(held, other, wide, adjoint):
@@ -346,17 +403,18 @@
     lax.fori_loop(0, STEPS // 2, pair, 0)
 
 
-def load_wide(field, held, send_sems, recv_sems, greet):
+def load_wide(field, held, send_sems, recv_sems, signal, wait):
     columns = field.shape[1]
+    lat_edges(held)
+    signal()
 
     def fill(row, carry):
         held[HROW + row, pl.ds(HLON, columns)] = field[row]
         return carry
 
     lax.fori_loop(0, held.shape[0] - 2 * HROW, fill, 0)
-    lat_edges(held)
     down, up, west, east = halo_copies(held, send_sems, recv_sems)
-    greet()
+    wait()
     lat_start(down, up)
     lat_wait(down, up)
     west.start()
@@ -365,10 +423,10 @@
     east.wait()
 
 
-def system_kernel(field, wide, adjoint_out, forward_out, energy_out, held, other, send_sems, recv_sems):
+def system_kernel(field, wide, adjoint_out, scaled_out, forward_out, energy_out, held, other, send_sems, recv_sems):
     rows, columns = held.shape[0], held.shape[1]
     own = columns - 2 * HLON
-    load_wide(field, held, send_sems, recv_sems, greet_near)
+    load_wide(field, held, send_sems, recv_sems, signal_near, wait_near)
     model_steps(held, other, wide, True)
 
     def scale(row, energy):
@@ -376,6 +434,7 @@
         scaled = deviation * deviation * value
         held[row] = scaled
         adjoint_out[row - HROW] = value[HLON : HLON + own]
+        scaled_out[row - HROW] = scaled[HLON : HLON + own]
         return energy + (scaled * value)[HLON : HLON + own]
 
     energy = lax.fori_loop(HROW, rows - HROW, scale, jnp.zeros((own, LANES), jnp.float32))
@@ -394,18 +453,20 @@
 
 
 def return_kernel(
-    rows, energy, matrix, start, packing, norm,
-    rows_out, direction, step_out, ratio_out, norm_out, square_out,
+    rows, energy, matrix, start, packing, norm, scaled,
+    rows_out, natural_out, direction, step_out, ratio_out, norm_out, square_out,
     sent, got, sent_next, got_next, send_sems, recv_sems, send_next, recv_next,
 ):
     slots, groups = rows.shape[:2]
     total = slots // DEPTH
     width = matrix.shape[0]
+    signal_all()
     for group in range(groups):
         sent[:, :, group * LANES : (group + 1) * LANES] = rows[:, group, :].reshape(total, DEPTH, LANES)
     sent[:, :, width:] = jnp.broadcast_to(energy[...][None], (total, DEPTH, LANES))
-    greet_all()
+    wait_all()
     trade_start(sent, got, send_sems, recv_sems)
+    unfold(scaled, natural_out)
     trade_wait(sent, got, send_sems, recv_sems)
     norm_first = norm[0:1, 0:1]
     step = norm_first / (norm_first + gathered_sum(got, width, 0))
@@ -430,24 +491,26 @@
 
 def last_kernel(
     field, wide, earlier, ratio, norm, square,
-    adjoint_out, step_out,
-    held, other, sent, got, halo_send, halo_recv, send_sems, recv_sems,
+    natural_out, step_out,
+    held, other, scaled, sent, got, halo_send, halo_recv, send_sems, recv_sems,
 ):
     rows, columns = held.shape[0], held.shape[1]
     own = columns - 2 * HLON
-    load_wide(field, held, halo_send, halo_recv, greet_all)
+    load_wide(field, held, halo_send, halo_recv, signal_all, wait_all)
     model_steps(held, other, wide, True)
     scale = ratio[0:1, 0:1]
 
     def combine(row, energy):
         value = held[HROW + row, pl.ds(HLON, own)] + scale * earlier[row]
-        adjoint_out[row] = value
-        deviation = wide[2, HROW + row, pl.ds(HLON, own)] * value
-        return energy + deviation * deviation
+        deviation = wide[2, HROW + row, pl.ds(HLON, own)]
+        product = deviation * deviation * value
+        scaled[row] = product
+        return energy + product * value
 
     energy = lax.fori_loop(0, rows - 2 * HROW, combine, jnp.zeros((own, LANES), jnp.float32))
     sent[...] = jnp.broadcast_to((full_sum(energy) + square[0:1, 0:1])[None], sent.shape)
     trade_start(sent, got, send_sems, recv_sems)
+    unfold(scaled, natural_out)
     trade_wait(sent, got, send_sems, recv_sems)
     step_out[...] = jnp.broadcast_to(norm[0:1, 0:1] / gathered_sum(got, 0, 0), step_out.shape)
 
@@ -470,20 +533,6 @@
     return pltpu.CompilerParams(
         collective_id=collective_id, has_side_effects=True, vmem_limit_bytes=LIMIT
     )
-
-
-def folded(values):
-    levels, columns, latitudes = values.shape
-    return (
-        values.reshape(levels, columns, latitudes // FOOT, FOOT)
-        .transpose(2, 1, 3, 0)
-        .reshape(latitudes // FOOT, columns, FOOT * levels)
-    )
-
-
-def unfolded(values, levels):
-    rows, columns, _ = values.shape
-    return values.reshape(rows, columns, FOOT, levels).transpose(3, 1, 0, 2).reshape(levels, columns, rows * FOOT)
 
 
 def body(
@@ -497,7 +546,6 @@
     slots = total * DEPTH
     groups = width // LANES
     wide_rows, wide_columns = rows + 2 * HROW, columns + 2 * HLON
-    fields = jnp.stack([folded(courant_lon), folded(courant_lat), folded(background_std)])
     spot = jnp.pad(
         jnp.stack([block_lon, block_lat], axis=1).astype(jnp.float32), ((0, 0), (0, LANES - 2))
     )
@@ -512,11 +560,11 @@
             shape(block_total, width), shape(slots, block_total), tile,
             shape(3, wide_rows, wide_columns, LANES),
         ),
-        in_specs=[smem()] + vmem(5),
+        in_specs=[smem()] + vmem(7),
         out_specs=tuple(vmem(7)),
         scratch_shapes=[chunks, chunks, dma((total,)), dma((total,)), dma((4,)), dma((4,))],
         compiler_params=params(0),
-    )(block_count, block_owner.reshape(1, block_total), spot, innovations, error_weight[0], fields)
+    )(block_count, block_owner.reshape(1, block_total), spot, innovations, error_weight[0], courant_lon, courant_lat, background_std)
 
     corners = jnp.concatenate([anchors[:, 0], anchors[:, 1]]).astype(jnp.int32)
 
@@ -530,11 +578,11 @@
         )(corners, block_rows)
 
     held = pltpu.VMEM((wide_rows, wide_columns, LANES), jnp.float32)
-    first, model_state, energy = pl.pallas_call(
+    first, scaled, model_state, energy = pl.pallas_call(
         system_kernel,
-        out_shape=(shape(rows, columns, LANES), shape(rows + 1, columns, LANES), tile),
+        out_shape=(shape(rows, columns, LANES), shape(rows, columns, LANES), shape(rows + 1, columns, LANES), tile),
         in_specs=vmem(2),
-        out_specs=tuple(vmem(3)),
+        out_specs=tuple(vmem(4)),
         scratch_shapes=[held, held, dma((4,)), dma((4,))],
         compiler_params=params(1),
     )(spread(arrived), wide)
@@ -547,29 +595,31 @@
         compiler_params=params(),
     )(corners, model_state)
 
-    arrived, direction, step_first, ratio, norm_next, square = pl.pallas_call(
+    arrived, first_part, direction, step_first, ratio, norm_next, square = pl.pallas_call(
         return_kernel,
-        out_shape=(shape(slots, groups, LANES), shape(block_total, width), tile, tile, tile, tile),
-        in_specs=vmem(6),
-        out_specs=tuple(vmem(6)),
+        out_shape=(
+            shape(slots, groups, LANES), shape(levels, columns, latitudes), shape(block_total, width),
+            tile, tile, tile, tile,
+        ),
+        in_specs=vmem(7),
+        out_specs=tuple(vmem(7)),
         scratch_shapes=[chunks, chunks, chunks, chunks] + [dma((total,))] * 4,
         compiler_params=params(2),
-    )(picked, energy, matrix, start, packing, norm)
+    )(picked, energy, matrix, start, packing, norm, scaled)
 
     tiles = pltpu.VMEM((total, DEPTH, LANES), jnp.float32)
-    second, step_second = pl.pallas_call(
+    second_part, step_second = pl.pallas_call(
         last_kernel,
-        out_shape=(shape(rows, columns, LANES), tile),
+        out_shape=(shape(levels, columns, latitudes), tile),
         in_specs=vmem(6),
         out_specs=tuple(vmem(2)),
-        scratch_shapes=[held, held, tiles, tiles, dma((4,)), dma((4,)), dma((total,)), dma((total,))],
+        scratch_shapes=[held, held, pltpu.VMEM((rows, columns, LANES), jnp.float32), tiles, tiles, dma((4,)), dma((4,)), dma((total,)), dma((total,))],
         compiler_params=params(3),
     )(spread(arrived), wide, first, ratio, norm_next, square)
 
     step_first, step_second = step_first[0, 0], step_second[0, 0]
     solution = step_first * start + step_second * direction
-    increment = unfolded(step_first * first + step_second * second, levels)
-    return solution, background_std * background_std * increment
+    return solution, step_first * first_part + step_second * second_part
 
 
 def solution(mesh):

time: 203 us -> 153 us (0.75)
  Pallas kernels: 163 us -> 137 us
  local copies, waits for them, and re-layouts: 29.3 us -> 9.37 us
  other arithmetic: 8.69 us -> 4.81 us
    pallas_call x1, Pallas kernels: 38.7 us -> 24.4 us  [body(): pl.pallas_call(system_kernel, out_shape=(shape(rows, columns, LANES), sha...]
    pallas_call x1, Pallas kernels: 32.7 us -> 25.1 us  [body(): pl.pallas_call(last_kernel, out_shape=(shape(levels, columns, latitudes),...]
    unnamed x16, local copies, waits for them, and re-layouts: 15.3 us -> 7.96 us
    another operation x3 -> x0, local copies, waits for them, and re-layouts: 5.75 us -> none  [body(): jnp.stack([folded(courant_lon), folded(courant_lat), folded(background_st...]
    pallas_call x2, Pallas kernels: 12.4 us -> 8.11 us  [spread(): pl.pallas_call(spread_kernel, out_shape=shape(rows + 1, columns, LANES),...]
    transpose x1 -> x0, local copies, waits for them, and re-layouts: 4.28 us -> none  [unfolded(): values.reshape(rows, columns, FOOT, levels).transpose(3, 1, 0, 2)]
    mul x1 -> x0, other arithmetic: 3.42 us -> none  [body(): return (solution, background_std * background_std * increment)]
    reshape x1 -> x0, local copies, waits for them, and re-layouts: 2.62 us -> none  [unfolded(): values.reshape(rows, columns, FOOT, levels).transpose(3, 1, 0, 2)]
where the time goes in v3:
time: 153 us
  Pallas kernels  137 us (90%)
  local copies, waits for them, and re-layouts  9.37 us (6%)
  other arithmetic  4.81 us (3%)
    pallas_call x1, Pallas kernels, body(): pl.pallas_call(return_kernel, out_shape=(shape(slots, groups, LANES), sha...  39 us
    pallas_call x1, Pallas kernels, body(): pl.pallas_call(first_kernel, out_shape=(shape(slots, groups, LANES), shap...  36.9 us
    pallas_call x1, Pallas kernels, body(): pl.pallas_call(last_kernel, out_shape=(shape(levels, columns, latitudes),...  25.1 us
    pallas_call x1, Pallas kernels, body(): pl.pallas_call(system_kernel, out_shape=(shape(rows, columns, LANES), sha...  24.4 us
    pallas_call x2, Pallas kernels, spread(): pl.pallas_call(spread_kernel, out_shape=shape(rows + 1, columns, LANES),...  8.11 us
    unnamed x16, local copies, waits for them, and re-layouts  7.96 us
    pallas_call x1, Pallas kernels, body(): pl.pallas_call(sample_kernel, out_shape=shape(slots, groups, LANES), in_s...  3.77 us

profile of v3, /device:TPU:0, one launch (start us, length us, event | category | flops | bytes accessed | tf_op | source)
XLA Modules:
  0.0 152.8 jit_solution(951966084246949806)
XLA Ops:
  1.3 0.7 add_convert_fusion
  2.0 0.1 copy.16
  2.1 0.0 copy-start.2
  2.1 1.2 copy-done.2
  3.3 1.1 copy-done.3
  4.4 1.1 copy-done.4
  5.5 1.1 copy-done.5
  6.6 0.9 copy-done.6
  7.5 0.7 copy-done.7
  8.2 36.9 %shard_map.104 = (f32[256,4,128]{2,1,0:T(4,128)S(1)}, f32[256,128]{1,0:T(8,128)S(1)}, f32[512,512]{1,0:T(8,128)S(1)}, f32[128,512]{1,0:T(8,128)S(1)}, f32[256,12...) custom-call(s32[1]{0:T(128)S(6)} %copy.17.count, s32[1,128]{1,0:T(1,128)S(1)} %bitcast.7, ...), custom_call_target="tpu_custom_call" | custom-call | tf_op jit(solution)/shard_map/pallas_call | solution.py:556
  45.1 0.2 slice_reduce_fusion.1
  45.3 4.1 %shard_map.105.field = f32[33,40,128]{2,1,0:T(8,128)S(1)} custom-call(s32[512]{0:T(512)S(1)} %maximum_convert_fusion.anchors, f32[256,4,128]{2,1,0:T(4,128)S(1)} %get-tuple-element.23.rows), custom_call_target="tpu_custom_call" | custom-call | tf_op jit(solution)/shard_map/pallas_call | solution.py:572
  49.4 1.9 %copy-done = f32[3,36,56,128]{3,2,1,0:T(8,128)S(1)} copy-done((f32[3,36,56,128]{3,2,1,0:T(8,128)S(1)}, f32[3,36,56,128]{3,2,1,0:T(8,128)}, u32[]{:S(2)}) %copy-start) | copy-done | bytes 3096600
  51.3 24.4 %shard_map.106 = (f32[32,40,128]{2,1,0:T(8,128)S(1)}, f32[32,40,128]{2,1,0:T(8,128)S(1)}, f32[33,40,128]{2,1,0:T(8,128)S(1)}, f32[8,128]{1,0:T(8,128)S(1)}) custom-call(f32[33,40,128]{2,1,0:T(8,128)S(1)} %shard_map.105.field, f32[3,36,56,128]{3,2,1,0:T(8,128)S(1)} %copy-done), custom_call_target="tpu_custom_call" | custom-call | tf_op jit(solution)/shard_map/pallas_call | solution.py:581
  75.6 0.0 copy-start.1
  75.6 3.8 %shard_map.107.rows = f32[256,4,128]{2,1,0:T(4,128)S(1)} custom-call(s32[512]{0:T(512)S(1)} %maximum_convert_fusion.anchors, f32[33,40,128]{2,1,0:T(8,128)S(1)} %get-tuple-element.25.field), custom_call_target="tpu_custom_call" | custom-call | tf_op jit(solution)/shard_map/pallas_call | solution.py:590
  79.4 39.0 %shard_map.108 = (f32[256,4,128]{2,1,0:T(4,128)S(1)}, f32[32,40,128]{2,1,0:T(8,128)S(1)}, f32[128,512]{1,0:T(8,128)S(1)}, f32[8,128]{1,0:T(8,128)S(1)}, f32[8,12...) custom-call(f32[256,4,128]{2,1,0:T(4,128)S(1)} %shard_map.107.rows, ...), custom_call_target="tpu_custom_call" | custom-call | tf_op jit(solution)/shard_map/pallas_call | solution.py:598
  118.4 0.6 slice.14
  119.0 4.1 %shard_map.109.field = f32[33,40,128]{2,1,0:T(8,128)S(1)} custom-call(s32[512]{0:T(512)S(1)} %maximum_convert_fusion.anchors, f32[256,4,128]{2,1,0:T(4,128)S(1)} %get-tuple-element.33.rows), custom_call_target="tpu_custom_call" | custom-call | tf_op jit(solution)/shard_map/pallas_call | solution.py:572
  123.1 0.0 copy-done.1
  123.1 25.1 %shard_map.110 = (f32[32,40,128]{2,1,0:T(8,128)S(1)}, f32[8,128]{1,0:T(8,128)S(1)}) custom-call(f32[33,40,128]{2,1,0:T(8,128)S(1)} %shard_map.109.field, f32[3,36,56,128]{3,2,1,0:T(8,128)S(1)} %copy-done.1, f32[32,40,128]{2,1,0:T(8,128)S(1)} %get-tuple-element.34.earlier, f32[8,128]{1,0:T(8,128)S(1)} %get-tuple-element.35.ratio, ...), custom_call_target="tpu_custom_call" | custom-call | tf_op jit(solution)/shard_map/pallas_call | solution.py:611
  148.2 0.5 slice.15
  148.7 2.1 %multiply_add_fusion = f32[32,40,128]{2,1,0:T(8,128)} fusion(f32[32,40,128]{2,1,0:T(8,128)S(1)} %get-tuple-element.41, f32[32,40,128]{2,1,0:T(8,128)S(1)} %get-tuple-element.40, f32[]{:T(128)} %bitcast.5, f32[]{:T(128)} %bitcast.4), kind=kLoop, calls=%fused_computation | loop fusion | flops 491520 | bytes 1966088 | tf_op jit(solution)/shard_map/add | solution.py:622
  150.8 2.0 %multiply_add_fusion.1 = f32[128,512]{1,0:T(8,128)} fusion(f32[128,512]{1,0:T(8,128)S(1)} %get-tuple-element.39, f32[128,512]{1,0:T(8,128)S(1)} %get-tuple-element.28.start, f32[]{:T(128)} %bitcast.5, f32[]{:T(128)} %bitcast.4), kind=kLoop, calls=%fused_computation.1 | loop fusion | flops 196608 | bytes 786440 | tf_op jit(solution)/shard_map/add | solution.py:621
  (8 shorter events, 0.0 us)
Async XLA Ops:
  2.1 1.2 copy-start.2
  3.3 1.1 copy-start.3
  4.4 1.1 copy-start.4
  5.5 1.1 copy-start.5
  6.6 0.9 copy-start.6
  7.5 0.7 copy-start.7
  49.4 1.9 %copy-start = (f32[3,36,56,128]{3,2,1,0:T(8,128)S(1)}, f32[3,36,56,128]{3,2,1,0:T(8,128)}, u32[]{:S(2)}) copy-start(f32[3,36,56,128]{3,2,1,0:T(8,128)} %get-tuple-element.24.wide) | copy-start | bytes 9289732
  75.6 47.4 %copy-start.1 = (f32[3,36,56,128]{3,2,1,0:T(8,128)S(1)}, f32[3,36,56,128]{3,2,1,0:T(8,128)}, u32[]{:S(2)}) copy-start(f32[3,36,56,128]{3,2,1,0:T(8,128)} %get-tuple-element.24.wide) | copy-start | bytes 9289732

commit v4 on v3

--- a/solution.py
+++ b/solution.py
@@ -198,8 +198,8 @@
     return jnp.sum(jnp.sum(values, axis=0, keepdims=True), axis=1, keepdims=True)
 
 
-def gathered_sum(got, first, lane_index):
-    tile = jnp.sum(got[:, :, first : first + LANES], axis=0)
+def gathered_sum(got, lane_index):
+    tile = jnp.sum(got[...], axis=0)
     lane = lax.broadcasted_iota(jnp.int32, tile.shape, 1)
     row = lax.broadcasted_iota(jnp.int32, tile.shape, 0)
     return full_sum(jnp.where((lane == lane_index) & (row == 0), tile, 0.0))
@@ -225,20 +225,21 @@
     return grouped
 
 
-def fold(natural, store):
-    levels, columns, latitudes = natural.shape
+def fold(fields, store):
+    count, levels, columns, latitudes = fields.shape
     rows = latitudes // FOOT
     choose = chooser(latitudes)
 
     def group(index, carry):
-        stack = jnp.concatenate([natural[:, FOOT * index + i, :] for i in range(FOOT)], axis=0)
-        mixed = dot(choose, stack, ((1,), (1,)))
-        pieces = [[mixed[q * rows : (q + 1) * rows]] * FOOT for q in range(FOOT)]
-        for i, value in enumerate(regroup(pieces, levels)):
-            store(FOOT * index + i, value)
-        return carry
-
-    lax.fori_loop(0, columns // FOOT, group, 0)
+        for field in range(count):
+            stack = jnp.concatenate([fields[field, :, FOOT * index + i, :] for i in range(FOOT)], axis=0)
+            mixed = dot(choose, stack, ((1,), (1,)))
+            pieces = [[mixed[q * rows : (q + 1) * rows]] * FOOT for q in range(FOOT)]
+            for i, value in enumerate(regroup(pieces, levels)):
+                store(field, FOOT * index + i, value)
+        return carry
+
+    lax.fori_loop(0, columns // FOOT, group, 0, unroll=2)
 
 
 def unfold(folded, natural):
@@ -253,28 +254,38 @@
             natural[:, FOOT * index + i, :] = stack[i * levels : (i + 1) * levels]
         return carry
 
-    lax.fori_loop(0, columns // FOOT, group, 0)
+    lax.fori_loop(0, columns // FOOT, group, 0, unroll=5)
 
 
 def first_kernel(
     count, owner, spot, innovations, matrix, courant_lon, courant_lat, deviation,
     rows_out, anchors_out, permuted, residual, packing, norm_out, wide,
-    sent, got, send_sems, recv_sems, halo_send, halo_recv,
+    sent, got, note, got_note, held_matrix, held_fields,
+    send_sems, recv_sems, note_send, note_recv, halo_send, halo_recv, load_sems,
 ):
     slots, block_total = packing.shape
     total = slots // DEPTH
     width = matrix.shape[0]
+    matrix_copy = pltpu.make_async_copy(matrix, held_matrix, load_sems.at[3])
+    matrix_copy.start()
+    field_copies = [
+        pltpu.make_async_copy(natural, held_fields.at[index], load_sems.at[index])
+        for index, natural in enumerate((courant_lon, courant_lat, deviation))
+    ]
+    for copy in field_copies:
+        copy.start()
     lat_edges(wide)
     signal_all()
+    matrix_copy.wait()
     live_column = lax.broadcasted_iota(jnp.int32, (block_total, 1), 0) < count[0]
-    start = jnp.where(live_column, dot(innovations[...], matrix[...], ((1,), (1,))), 0.0)
+    start = jnp.where(live_column, dot(innovations[...], held_matrix[...], ((1,), (1,))), 0.0)
     residual[...] = start
     row = lax.broadcasted_iota(jnp.int32, (width, width), 0)
     column = lax.broadcasted_iota(jnp.int32, (width, width), 1)
     footprint = FOOT * FOOT
     shuffle = column == lax.rem(row, footprint) * (width // footprint) + lax.div(row, footprint)
     shuffle = shuffle.astype(jnp.float32)
-    weighted = dot(dot(start, matrix[...]), shuffle)
+    weighted = dot(dot(start, held_matrix[...]), shuffle)
 
     live_row = lax.broadcasted_iota(jnp.int32, (1, block_total), 1) < count[0]
     owners = owner[...]
@@ -288,28 +299,34 @@
     slot_ids = lax.broadcasted_iota(jnp.int32, (slots, block_total), 0).astype(jnp.float32)
     pack = jnp.where((slot_ids == target) & live_row, 1.0, 0.0)
     packing[...] = pack
-    sent[:, :, :width] = dot(pack, weighted).reshape(total, DEPTH, width)
-    lane = lax.broadcasted_iota(jnp.int32, (slots, LANES), 1)
-    spots = jnp.where(lane == 2, full_sum(start * start), dot(pack, spot[...]))
-    sent[:, :, width:] = spots.reshape(total, DEPTH, LANES)
+    sent[...] = dot(pack, weighted).reshape(total, DEPTH, width)
+    spots = dot(pack, spot[...]).reshape(total, DEPTH, LANES)
+    lane = lax.broadcasted_iota(jnp.int32, spots.shape, 2)
+    depth = lax.broadcasted_iota(jnp.int32, spots.shape, 1)
+    spots = jnp.sum(jnp.where(lax.rem(lane, DEPTH) == depth, spots, 0.0), axis=1, keepdims=True)
+    lane = lax.broadcasted_iota(jnp.int32, spots.shape, 2)
+    note[...] = jnp.where(lane == 2 * DEPTH, full_sum(start * start)[None], spots)
     wait_all()
     trade_start(sent, got, send_sems, recv_sems)
-    for index, natural in enumerate((courant_lon, courant_lat, deviation)):
-
-        def store(place_in, value, index=index):
-            wide[index, pl.ds(HROW, value.shape[0]), HLON + place_in, :] = value
-
-        fold(natural, store)
+    trade_start(note, got_note, note_send, note_recv)
+    for copy in field_copies:
+        copy.wait()
+
+    def store(index, column, value):
+        wide[index, pl.ds(HROW, value.shape[0]), HLON + column, :] = value
+
+    fold(held_fields, store)
     down, up, west, east = halo_copies(wide, halo_send, halo_recv)
     lat_start(down, up)
-    permuted[...] = dot(matrix[...], shuffle)
+    permuted[...] = dot(held_matrix[...], shuffle)
     lat_wait(down, up)
     west.start()
     east.start()
     trade_wait(sent, got, send_sems, recv_sems)
+    trade_wait(note, got_note, note_send, note_recv)
     unload(got, rows_out)
-    anchors_out[...] = got[:, :, width:].reshape(slots, LANES)
-    norm_out[...] = jnp.broadcast_to(gathered_sum(got, width, 2), norm_out.shape)
+    anchors_out[...] = got_note[...].reshape(total, LANES)
+    norm_out[...] = jnp.broadcast_to(gathered_sum(got_note, 2 * DEPTH), norm_out.shape)
     west.wait()
     east.wait()
 
@@ -335,7 +352,7 @@
         field[row + 1, pl.ds(column, FOOT), :] += jnp.where(here, 0.0, patch)
         return carry
 
-    lax.fori_loop(0, slots, add, 0, unroll=8)
+    lax.fori_loop(0, slots, add, 0, unroll=16)
 
 
 def sample_kernel(anchors, field, rows):
@@ -351,7 +368,7 @@
         rows[slot] = pltpu.roll(jnp.where(lane >= shift, here, after), lax.rem(LANES - shift, LANES), 1)
         return carry
 
-    lax.fori_loop(0, slots, pick, 0, unroll=8)
+    lax.fori_loop(0, slots, pick, 0, unroll=16)
 
 
 def model_step(now, later, wide, adjoint):
@@ -455,7 +472,8 @@
 def return_kernel(
     rows, energy, matrix, start, packing, norm, scaled,
     rows_out, natural_out, direction, step_out, ratio_out, norm_out, square_out,
-    sent, got, sent_next, got_next, send_sems, recv_sems, send_next, recv_next,
+    sent, got, sent_next, got_next, note, got_note, note_next, got_note_next,
+    send_sems, recv_sems, send_next, recv_next, note_send, note_recv, note_send_next, note_recv_next,
 ):
     slots, groups = rows.shape[:2]
     total = slots // DEPTH
@@ -463,23 +481,27 @@
     signal_all()
     for group in range(groups):
         sent[:, :, group * LANES : (group + 1) * LANES] = rows[:, group, :].reshape(total, DEPTH, LANES)
-    sent[:, :, width:] = jnp.broadcast_to(energy[...][None], (total, DEPTH, LANES))
+    note[...] = jnp.broadcast_to(energy[0:1][None], note.shape)
     wait_all()
     trade_start(sent, got, send_sems, recv_sems)
+    trade_start(note, got_note, note_send, note_recv)
     unfold(scaled, natural_out)
     trade_wait(sent, got, send_sems, recv_sems)
+    trade_wait(note, got_note, note_send, note_recv)
     norm_first = norm[0:1, 0:1]
-    step = norm_first / (norm_first + gathered_sum(got, width, 0))
-    back = dot(packing[...], got[:, :, :width].reshape(slots, width), ((0,), (0,)))
+    step = norm_first / (norm_first + gathered_sum(got_note, 0))
+    back = dot(packing[...], got[...].reshape(slots, width), ((0,), (0,)))
     image = start[...] + dot(back, matrix[...], ((1,), (1,)))
     residual = start[...] - step * image
     pack = packing[...]
-    sent_next[:, :, :width] = dot(pack, dot(residual, matrix[...])).reshape(total, DEPTH, width)
-    sent_next[:, :, width:] = jnp.broadcast_to(full_sum(residual * residual)[None], (total, DEPTH, LANES))
+    sent_next[...] = dot(pack, dot(residual, matrix[...])).reshape(total, DEPTH, width)
+    note_next[...] = jnp.broadcast_to(full_sum(residual * residual)[None], note_next.shape)
     trade_start(sent_next, got_next, send_next, recv_next)
+    trade_start(note_next, got_note_next, note_send_next, note_recv_next)
     trade_wait(sent_next, got_next, send_next, recv_next)
+    trade_wait(note_next, got_note_next, note_send_next, note_recv_next)
     unload(got_next, rows_out)
-    norm_next = gathered_sum(got_next, width, 0)
+    norm_next = gathered_sum(got_note_next, 0)
     ratio = norm_next / norm_first
     moved = residual + ratio * start[...]
     direction[...] = moved
@@ -512,7 +534,7 @@
     trade_start(sent, got, send_sems, recv_sems)
     unfold(scaled, natural_out)
     trade_wait(sent, got, send_sems, recv_sems)
-    step_out[...] = jnp.broadcast_to(norm[0:1, 0:1] / gathered_sum(got, 0, 0), step_out.shape)
+    step_out[...] = jnp.broadcast_to(norm[0:1, 0:1] / gathered_sum(got, 0), step_out.shape)
 
 
 def vmem(count):
@@ -547,26 +569,33 @@
     groups = width // LANES
     wide_rows, wide_columns = rows + 2 * HROW, columns + 2 * HLON
     spot = jnp.pad(
-        jnp.stack([block_lon, block_lat], axis=1).astype(jnp.float32), ((0, 0), (0, LANES - 2))
+        jnp.repeat(jnp.stack([block_lon, block_lat], axis=1), DEPTH, axis=1).astype(jnp.float32),
+        ((0, 0), (0, LANES - 2 * DEPTH)),
     )
     tile = shape(DEPTH, LANES)
-    chunks = pltpu.VMEM((total, DEPTH, width + LANES), jnp.float32)
+    chunks = pltpu.VMEM((total, DEPTH, width), jnp.float32)
+    notes = pltpu.VMEM((total, 1, LANES), jnp.float32)
     dma = pltpu.SemaphoreType.DMA
 
     arrived, anchors, matrix, start, packing, norm, wide = pl.pallas_call(
         first_kernel,
         out_shape=(
-            shape(slots, groups, LANES), shape(slots, LANES), shape(width, width),
+            shape(slots, groups, LANES), shape(total, LANES), shape(width, width),
             shape(block_total, width), shape(slots, block_total), tile,
             shape(3, wide_rows, wide_columns, LANES),
         ),
-        in_specs=[smem()] + vmem(7),
+        in_specs=[smem()] + vmem(3) + [pl.BlockSpec(memory_space=pl.ANY)] * 4,
         out_specs=tuple(vmem(7)),
-        scratch_shapes=[chunks, chunks, dma((total,)), dma((total,)), dma((4,)), dma((4,))],
+        scratch_shapes=[
+            chunks, chunks, notes, notes,
+            pltpu.VMEM((width, width), jnp.float32),
+            pltpu.VMEM((3, levels, columns, latitudes), jnp.float32),
+            *[dma((total,))] * 4, dma((4,)), dma((4,)), dma((4,)),
+        ],
         compiler_params=params(0),
     )(block_count, block_owner.reshape(1, block_total), spot, innovations, error_weight[0], courant_lon, courant_lat, background_std)
 
-    corners = jnp.concatenate([anchors[:, 0], anchors[:, 1]]).astype(jnp.int32)
+    corners = anchors[:, : 2 * DEPTH].reshape(total, 2, DEPTH).transpose(1, 0, 2).reshape(-1).astype(jnp.int32)
 
     def spread(block_rows):
         return pl.pallas_call(
@@ -603,17 +632,16 @@
         ),
         in_specs=vmem(7),
         out_specs=tuple(vmem(7)),
-        scratch_shapes=[chunks, chunks, chunks, chunks] + [dma((total,))] * 4,
+        scratch_shapes=[chunks] * 4 + [notes] * 4 + [dma((total,))] * 8,
         compiler_params=params(2),
     )(picked, energy, matrix, start, packing, norm, scaled)
 
-    tiles = pltpu.VMEM((total, DEPTH, LANES), jnp.float32)
     second_part, step_second = pl.pallas_call(
         last_kernel,
         out_shape=(shape(levels, columns, latitudes), tile),
         in_specs=vmem(6),
         out_specs=tuple(vmem(2)),
-        scratch_shapes=[held, held, pltpu.VMEM((rows, columns, LANES), jnp.float32), tiles, tiles, dma((4,)), dma((4,)), dma((total,)), dma((total,))],
+        scratch_shapes=[held, held, pltpu.VMEM((rows, columns, LANES), jnp.float32), notes, notes, dma((4,)), dma((4,)), dma((total,)), dma((total,))],
         compiler_params=params(3),
     )(spread(arrived), wide, first, ratio, norm_next, square)
 

time: 153 us -> 144 us (0.941)
  Pallas kernels: 137 us -> 128 us
    pallas_call x1, Pallas kernels: 36.9 us -> 31.7 us  [body(): pl.pallas_call(first_kernel, out_shape=(shape(slots, groups, LANES), shap...]
    pallas_call x2, Pallas kernels: 8.11 us -> 6.04 us  [spread(): pl.pallas_call(spread_kernel, out_shape=shape(rows + 1, columns, LANES),...]
    pallas_call x1, Pallas kernels: 25.1 us -> 23.1 us  [body(): pl.pallas_call(last_kernel, out_shape=(shape(levels, columns, latitudes),...]
where the time goes in v4:
time: 144 us
  Pallas kernels  128 us (89%)
  local copies, waits for them, and re-layouts  9.44 us (7%)
  other arithmetic  4.85 us (3%)
    pallas_call x1, Pallas kernels, body(): pl.pallas_call(return_kernel, out_shape=(shape(slots, groups, LANES), sha...  38.5 us
    pallas_call x1, Pallas kernels, body(): pl.pallas_call(first_kernel, out_shape=(shape(slots, groups, LANES), shap...  31.7 us
    pallas_call x1, Pallas kernels, body(): pl.pallas_call(system_kernel, out_shape=(shape(rows, columns, LANES), sha...  25.6 us
    pallas_call x1, Pallas kernels, body(): pl.pallas_call(last_kernel, out_shape=(shape(levels, columns, latitudes),...  23.1 us
    unnamed x16, local copies, waits for them, and re-layouts  7.96 us
    pallas_call x2, Pallas kernels, spread(): pl.pallas_call(spread_kernel, out_shape=shape(rows + 1, columns, LANES),...  6.04 us
    pallas_call x1, Pallas kernels, body(): pl.pallas_call(sample_kernel, out_shape=shape(slots, groups, LANES), in_s...  2.97 us

profile of v4, /device:TPU:0, one launch (start us, length us, event | category | flops | bytes accessed | tf_op | source)
XLA Modules:
  0.0 143.6 jit_solution(11151170453633893292)
XLA Ops:
  1.3 0.7 add_convert_fusion
  2.0 0.1 copy.15
  2.1 0.0 copy-start.2
  2.1 1.2 copy-done.2
  3.3 1.1 copy-done.3
  4.4 1.1 copy-done.4
  5.5 1.1 copy-done.5
  6.6 0.9 copy-done.6
  7.5 0.7 copy-done.7
  8.2 31.7 %shard_map.104 = (f32[256,4,128]{2,1,0:T(4,128)S(1)}, f32[32,128]{1,0:T(8,128)S(1)}, f32[512,512]{1,0:T(8,128)S(1)}, f32[128,512]{1,0:T(8,128)S(1)}, f32[256,128...) custom-call(s32[1]{0:T(128)S(6)} %copy.18.count, s32[1,128]{1,0:T(1,128)S(1)} %bitcast.12, ...), custom_call_target="tpu_custom_call" | custom-call | tf_op jit(solution)/shard_map/pallas_call | solution.py:580
  39.9 0.1 copy.16
  40.0 0.1 copy.17
  40.1 0.1 convert_element_type.23.anchors
  40.2 3.0 %shard_map.105.field = f32[33,40,128]{2,1,0:T(8,128)S(1)} custom-call(s32[512]{0:T(512)S(1)} %convert_element_type.23.anchors, f32[256,4,128]{2,1,0:T(4,128)S(1)} %get-tuple-element.23.rows), custom_call_target="tpu_custom_call" | custom-call | tf_op jit(solution)/shard_map/pallas_call | solution.py:601
  43.2 1.9 %copy-done = f32[3,36,56,128]{3,2,1,0:T(8,128)S(1)} copy-done((f32[3,36,56,128]{3,2,1,0:T(8,128)S(1)}, f32[3,36,56,128]{3,2,1,0:T(8,128)}, u32[]{:S(2)}) %copy-start) | copy-done | bytes 3096600
  45.1 25.6 %shard_map.106 = (f32[32,40,128]{2,1,0:T(8,128)S(1)}, f32[32,40,128]{2,1,0:T(8,128)S(1)}, f32[33,40,128]{2,1,0:T(8,128)S(1)}, f32[8,128]{1,0:T(8,128)S(1)}) custom-call(f32[33,40,128]{2,1,0:T(8,128)S(1)} %shard_map.105.field, f32[3,36,56,128]{3,2,1,0:T(8,128)S(1)} %copy-done), custom_call_target="tpu_custom_call" | custom-call | tf_op jit(solution)/shard_map/pallas_call | solution.py:610
  70.7 3.0 %shard_map.107.rows = f32[256,4,128]{2,1,0:T(4,128)S(1)} custom-call(s32[512]{0:T(512)S(1)} %convert_element_type.23.anchors, f32[33,40,128]{2,1,0:T(8,128)S(1)} %get-tuple-element.25.field), custom_call_target="tpu_custom_call" | custom-call | tf_op jit(solution)/shard_map/pallas_call | solution.py:619
  73.7 38.5 %shard_map.108 = (f32[256,4,128]{2,1,0:T(4,128)S(1)}, f32[32,40,128]{2,1,0:T(8,128)S(1)}, f32[128,512]{1,0:T(8,128)S(1)}, f32[8,128]{1,0:T(8,128)S(1)}, f32[8,12...) custom-call(f32[256,4,128]{2,1,0:T(4,128)S(1)} %shard_map.107.rows, ...), custom_call_target="tpu_custom_call" | custom-call | tf_op jit(solution)/shard_map/pallas_call | solution.py:627
  112.2 0.5 slice.10
  112.7 3.0 %shard_map.109.field = f32[33,40,128]{2,1,0:T(8,128)S(1)} custom-call(s32[512]{0:T(512)S(1)} %convert_element_type.23.anchors, f32[256,4,128]{2,1,0:T(4,128)S(1)} %get-tuple-element.33.rows), custom_call_target="tpu_custom_call" | custom-call | tf_op jit(solution)/shard_map/pallas_call | solution.py:601
  115.8 23.1 %shard_map.110 = (f32[32,40,128]{2,1,0:T(8,128)S(1)}, f32[8,128]{1,0:T(8,128)S(1)}) custom-call(f32[33,40,128]{2,1,0:T(8,128)S(1)} %shard_map.109.field, f32[3,36,56,128]{3,2,1,0:T(8,128)S(1)} %copy-done.1, f32[32,40,128]{2,1,0:T(8,128)S(1)} %get-tuple-element.34.earlier, f32[8,128]{1,0:T(8,128)S(1)} %get-tuple-element.35.ratio, ...), custom_call_target="tpu_custom_call" | custom-call | tf_op jit(solution)/shard_map/pallas_call | solution.py:639
  138.9 0.6 slice.11
  139.5 2.2 %multiply_add_fusion = f32[32,40,128]{2,1,0:T(8,128)} fusion(f32[32,40,128]{2,1,0:T(8,128)S(1)} %get-tuple-element.41, f32[32,40,128]{2,1,0:T(8,128)S(1)} %get-tuple-element.40, f32[]{:T(128)} %bitcast.8, f32[]{:T(128)} %bitcast.7), kind=kLoop, calls=%fused_computation | loop fusion | flops 491520 | bytes 1966088 | tf_op jit(solution)/shard_map/add | solution.py:650
  141.6 2.0 %multiply_add_fusion.1 = f32[128,512]{1,0:T(8,128)} fusion(f32[128,512]{1,0:T(8,128)S(1)} %get-tuple-element.39, f32[128,512]{1,0:T(8,128)S(1)} %get-tuple-element.28.start, f32[]{:T(128)} %bitcast.8, f32[]{:T(128)} %bitcast.7), kind=kLoop, calls=%fused_computation.1 | loop fusion | flops 196608 | bytes 786440 | tf_op jit(solution)/shard_map/add | solution.py:649
  (11 shorter events, 0.0 us)
Async XLA Ops:
  2.1 1.2 copy-start.2
  3.3 1.1 copy-start.3
  4.4 1.1 copy-start.4
  5.5 1.1 copy-start.5
  6.6 0.9 copy-start.6
  7.5 0.7 copy-start.7
  43.2 1.9 %copy-start = (f32[3,36,56,128]{3,2,1,0:T(8,128)S(1)}, f32[3,36,56,128]{3,2,1,0:T(8,128)}, u32[]{:S(2)}) copy-start(f32[3,36,56,128]{3,2,1,0:T(8,128)} %get-tuple-element.24.wide) | copy-start | bytes 9289732
  70.7 45.1 %copy-start.1 = (f32[3,36,56,128]{3,2,1,0:T(8,128)S(1)}, f32[3,36,56,128]{3,2,1,0:T(8,128)}, u32[]{:S(2)}) copy-start(f32[3,36,56,128]{3,2,1,0:T(8,128)} %get-tuple-element.24.wide) | copy-start | bytes 9289732

commit v5 on v4

--- a/solution.py
+++ b/solution.py
@@ -47,24 +47,28 @@
     pl.semaphore_wait(pltpu.get_barrier_semaphore(), lat_n * lon_n - 1)
 
 
+def ways():
+    return [(dlat, dlon) for dlat in (-1, 0, 1) for dlon in (-1, 0, 1) if dlat or dlon]
+
+
+def inside(dlat, lat_i, lat_n):
+    return (lat_i + dlat >= 0) & (lat_i + dlat < lat_n)
+
+
 def signal_near():
     lat_n, lon_n, lat_i, lon_i = place()
     barrier = pltpu.get_barrier_semaphore()
-    for near in (lax.rem(lon_i + 1, lon_n), lax.rem(lon_i + lon_n - 1, lon_n)):
-        pl.semaphore_signal(barrier, inc=1, device_id=(lat_i, near), device_id_type=MESH)
-
-    @pl.when(lat_i > 0)
-    def _():
-        pl.semaphore_signal(barrier, inc=1, device_id=(lat_i - 1, lon_i), device_id_type=MESH)
-
-    @pl.when(lat_i < lat_n - 1)
-    def _():
-        pl.semaphore_signal(barrier, inc=1, device_id=(lat_i + 1, lon_i), device_id_type=MESH)
+    for dlat, dlon in ways():
+
+        @pl.when(inside(dlat, lat_i, lat_n))
+        def _(dlat=dlat, dlon=dlon):
+            device = (lat_i + dlat, lax.rem(lon_i + lon_n + dlon, lon_n))
+            pl.semaphore_signal(barrier, inc=1, device_id=device, device_id_type=MESH)
 
 
 def wait_near():
     lat_n, lon_n, lat_i, lon_i = place()
-    peers = 2 + jnp.where(lat_i > 0, 1, 0) + jnp.where(lat_i < lat_n - 1, 1, 0)
+    peers = 2 + jnp.where(lat_i > 0, 3, 0) + jnp.where(lat_i < lat_n - 1, 3, 0)
     pl.semaphore_wait(pltpu.get_barrier_semaphore(), peers)
 
 
@@ -116,34 +120,50 @@
 
 def halo_copies(wide, send_sems, recv_sems):
     lat_n, lon_n, lat_i, lon_i = place()
-    rows, columns = wide.shape[-3], wide.shape[-2]
-    inner = (HLON, columns - 2 * HLON)
-
-    def copy(index, source, target, device):
-        return pltpu.make_async_remote_copy(
-            src_ref=source,
-            dst_ref=target,
+
+    def spans(step, length, halo):
+        if step < 0:
+            return (halo, halo), (length - halo, halo)
+        if step > 0:
+            return (length - 2 * halo, halo), (0, halo)
+        return (halo, length - 2 * halo), (halo, length - 2 * halo)
+
+    copies = []
+    for index, (dlat, dlon) in enumerate(ways()):
+        from_rows, to_rows = spans(dlat, wide.shape[-3], HROW)
+        from_columns, to_columns = spans(dlon, wide.shape[-2], HLON)
+        copy = pltpu.make_async_remote_copy(
+            src_ref=part(wide, from_rows, from_columns),
+            dst_ref=part(wide, to_rows, to_columns),
             send_sem=send_sems.at[index],
             recv_sem=recv_sems.at[index],
-            device_id=device,
+            device_id=(lat_i + dlat, lax.rem(lon_i + lon_n + dlon, lon_n)),
             device_id_type=MESH,
         )
-
-    down = copy(0, part(wide, (HROW, HROW), inner), part(wide, (rows - HROW, HROW), inner), (lat_i - 1, lon_i))
-    up = copy(1, part(wide, (rows - 2 * HROW, HROW), inner), part(wide, (0, HROW), inner), (lat_i + 1, lon_i))
-    west = copy(
-        2,
-        part(wide, (0, rows), (HLON, HLON)),
-        part(wide, (0, rows), (columns - HLON, HLON)),
-        (lat_i, lax.rem(lon_i + lon_n - 1, lon_n)),
-    )
-    east = copy(
-        3,
-        part(wide, (0, rows), (columns - 2 * HLON, HLON)),
-        part(wide, (0, rows), (0, HLON)),
-        (lat_i, lax.rem(lon_i + 1, lon_n)),
-    )
-    return down, up, west, east
+        copies.append((dlat, copy))
+    return copies
+
+
+def halo_start(copies):
+    lat_n, lon_n, lat_i, lon_i = place()
+    for dlat, copy in copies:
+
+        @pl.when(inside(dlat, lat_i, lat_n))
+        def _(copy=copy):
+            copy.start()
+
+
+def halo_wait(copies):
+    lat_n, lon_n, lat_i, lon_i = place()
+    for dlat, copy in copies:
+
+        @pl.when(inside(dlat, lat_i, lat_n))
+        def _(copy=copy):
+            copy.wait_send()
+
+        @pl.when(inside(-dlat, lat_i, lat_n))
+        def _(copy=copy):
+            copy.wait_recv()
 
 
 def lat_edges(wide):
@@ -160,32 +180,6 @@
             else:
                 for row in range(HROW):
                     wide[first + row] = jnp.zeros(wide.shape[1:], jnp.float32)
-
-
-def lat_start(down, up):
-    lat_n, lon_n, lat_i, lon_i = place()
-
-    @pl.when(lat_i > 0)
-    def _():
-        down.start()
-
-    @pl.when(lat_i < lat_n - 1)
-    def _():
-        up.start()
-
-
-def lat_wait(down, up):
-    lat_n, lon_n, lat_i, lon_i = place()
-
-    @pl.when(lat_i > 0)
-    def _():
-        down.wait_send()
-        up.wait_recv()
-
-    @pl.when(lat_i < lat_n - 1)
-    def _():
-        up.wait_send()
-        down.wait_recv()
 
 
 def dot(left, right, axes=((1,), (0,))):
@@ -259,7 +253,7 @@
 
 def first_kernel(
     count, owner, spot, innovations, matrix, courant_lon, courant_lat, deviation,
-    rows_out, anchors_out, permuted, residual, packing, norm_out, wide,
+    rows_out, anchors_out, permuted, residual, packing, packed_out, norm_out, wide,
     sent, got, note, got_note, held_matrix, held_fields,
     send_sems, recv_sems, note_send, note_recv, halo_send, halo_recv, load_sems,
 ):
@@ -300,6 +294,7 @@
     pack = jnp.where((slot_ids == target) & live_row, 1.0, 0.0)
     packing[...] = pack
     sent[...] = dot(pack, weighted).reshape(total, DEPTH, width)
+    packed_out[...] = sent[...]
     spots = dot(pack, spot[...]).reshape(total, DEPTH, LANES)
     lane = lax.broadcasted_iota(jnp.int32, spots.shape, 2)
     depth = lax.broadcasted_iota(jnp.int32, spots.shape, 1)
@@ -316,19 +311,15 @@
         wide[index, pl.ds(HROW, value.shape[0]), HLON + column, :] = value
 
     fold(held_fields, store)
-    down, up, west, east = halo_copies(wide, halo_send, halo_recv)
-    lat_start(down, up)
+    copies = halo_copies(wide, halo_send, halo_recv)
+    halo_start(copies)
     permuted[...] = dot(held_matrix[...], shuffle)
-    lat_wait(down, up)
-    west.start()
-    east.start()
     trade_wait(sent, got, send_sems, recv_sems)
     trade_wait(note, got_note, note_send, note_recv)
     unload(got, rows_out)
     anchors_out[...] = got_note[...].reshape(total, LANES)
     norm_out[...] = jnp.broadcast_to(gathered_sum(got_note, 2 * DEPTH), norm_out.shape)
-    west.wait()
-    east.wait()
+    halo_wait(copies)
 
 
 def unload(got, rows_out):
@@ -430,20 +421,22 @@
         return carry
 
     lax.fori_loop(0, held.shape[0] - 2 * HROW, fill, 0)
-    down, up, west, east = halo_copies(held, send_sems, recv_sems)
+    copies = halo_copies(held, send_sems, recv_sems)
     wait()
-    lat_start(down, up)
-    lat_wait(down, up)
-    west.start()
-    east.start()
-    west.wait()
-    east.wait()
-
-
-def system_kernel(field, wide, adjoint_out, scaled_out, forward_out, energy_out, held, other, send_sems, recv_sems):
+    halo_start(copies)
+    halo_wait(copies)
+
+
+def system_kernel(
+    field, wide_in, adjoint_out, scaled_out, forward_out, energy_out,
+    held, other, wide, send_sems, recv_sems, load_sems,
+):
     rows, columns = held.shape[0], held.shape[1]
     own = columns - 2 * HLON
+    load = pltpu.make_async_copy(wide_in, wide, load_sems.at[0])
+    load.start()
     load_wide(field, held, send_sems, recv_sems, signal_near, wait_near)
+    load.wait()
     model_steps(held, other, wide, True)
 
     def scale(row, energy):
@@ -470,7 +463,7 @@
 
 
 def return_kernel(
-    rows, energy, matrix, start, packing, norm, scaled,
+    rows, energy, matrix, start, packing, packed, norm, scaled,
     rows_out, natural_out, direction, step_out, ratio_out, norm_out, square_out,
     sent, got, sent_next, got_next, note, got_note, note_next, got_note_next,
     send_sems, recv_sems, send_next, recv_next, note_send, note_recv, note_send_next, note_recv_next,
@@ -485,19 +478,23 @@
     wait_all()
     trade_start(sent, got, send_sems, recv_sems)
     trade_start(note, got_note, note_send, note_recv)
-    unfold(scaled, natural_out)
+    product = dot(matrix[...], matrix[...], ((0,), (0,)))
+    pack = packing[...]
+    filled = jnp.sum(pack, axis=1, keepdims=True) > 0.5
     trade_wait(sent, got, send_sems, recv_sems)
     trade_wait(note, got_note, note_send, note_recv)
     norm_first = norm[0:1, 0:1]
     step = norm_first / (norm_first + gathered_sum(got_note, 0))
-    back = dot(packing[...], got[...].reshape(slots, width), ((0,), (0,)))
+    returned = jnp.where(filled, got[...].reshape(slots, width), 0.0)
+    change = packed[...].reshape(slots, width) + dot(returned, product)
+    sent_next[...] = packed[...] - step * change.reshape(total, DEPTH, width)
+    trade_start(sent_next, got_next, send_next, recv_next)
+    back = dot(pack, returned, ((0,), (0,)))
     image = start[...] + dot(back, matrix[...], ((1,), (1,)))
     residual = start[...] - step * image
-    pack = packing[...]
-    sent_next[...] = dot(pack, dot(residual, matrix[...])).reshape(total, DEPTH, width)
     note_next[...] = jnp.broadcast_to(full_sum(residual * residual)[None], note_next.shape)
-    trade_start(sent_next, got_next, send_next, recv_next)
     trade_start(note_next, got_note_next, note_send_next, note_recv_next)
+    unfold(scaled, natural_out)
     trade_wait(sent_next, got_next, send_next, recv_next)
     trade_wait(note_next, got_note_next, note_send_next, note_recv_next)
     unload(got_next, rows_out)
@@ -539,6 +536,10 @@
 
 def vmem(count):
     return [pl.BlockSpec(memory_space=pltpu.VMEM)] * count
+
+
+def hbm(count):
+    return [pl.BlockSpec(memory_space=pltpu.HBM)] * count
 
 
 def smem():
@@ -577,20 +578,21 @@
     notes = pltpu.VMEM((total, 1, LANES), jnp.float32)
     dma = pltpu.SemaphoreType.DMA
 
-    arrived, anchors, matrix, start, packing, norm, wide = pl.pallas_call(
+    arrived, anchors, matrix, start, packing, packed, norm, wide = pl.pallas_call(
         first_kernel,
         out_shape=(
             shape(slots, groups, LANES), shape(total, LANES), shape(width, width),
-            shape(block_total, width), shape(slots, block_total), tile,
+            shape(block_total, width), shape(slots, block_total),
+            shape(total, DEPTH, width), tile,
             shape(3, wide_rows, wide_columns, LANES),
         ),
-        in_specs=[smem()] + vmem(3) + [pl.BlockSpec(memory_space=pl.ANY)] * 4,
-        out_specs=tuple(vmem(7)),
+        in_specs=[smem()] + vmem(3) + hbm(4),
+        out_specs=tuple(vmem(8)),
         scratch_shapes=[
             chunks, chunks, notes, notes,
             pltpu.VMEM((width, width), jnp.float32),
             pltpu.VMEM((3, levels, columns, latitudes), jnp.float32),
-            *[dma((total,))] * 4, dma((4,)), dma((4,)), dma((4,)),
+            *[dma((total,))] * 4, dma((8,)), dma((8,)), dma((4,)),
         ],
         compiler_params=params(0),
     )(block_count, block_owner.reshape(1, block_total), spot, innovations, error_weight[0], courant_lon, courant_lat, background_std)
@@ -610,9 +612,9 @@
     first, scaled, model_state, energy = pl.pallas_call(
         system_kernel,
         out_shape=(shape(rows, columns, LANES), shape(rows, columns, LANES), shape(rows + 1, columns, LANES), tile),
-        in_specs=vmem(2),
+        in_specs=vmem(1) + hbm(1),
         out_specs=tuple(vmem(4)),
-        scratch_shapes=[held, held, dma((4,)), dma((4,))],
+        scratch_shapes=[held, held, pltpu.VMEM((3, wide_rows, wide_columns, LANES), jnp.float32), dma((8,)), dma((8,)), dma((1,))],
         compiler_params=params(1),
     )(spread(arrived), wide)
 
@@ -630,18 +632,18 @@
             shape(slots, groups, LANES), shape(levels, columns, latitudes), shape(block_total, width),
             tile, tile, tile, tile,
         ),
-        in_specs=vmem(7),
+        in_specs=vmem(8),
         out_specs=tuple(vmem(7)),
         scratch_shapes=[chunks] * 4 + [notes] * 4 + [dma((total,))] * 8,
         compiler_params=params(2),
-    )(picked, energy, matrix, start, packing, norm, scaled)
+    )(picked, energy, matrix, start, packing, packed, norm, scaled)
 
     second_part, step_second = pl.pallas_call(
         last_kernel,
         out_shape=(shape(levels, columns, latitudes), tile),
         in_specs=vmem(6),
         out_specs=tuple(vmem(2)),
-        scratch_shapes=[held, held, pltpu.VMEM((rows, columns, LANES), jnp.float32), notes, notes, dma((4,)), dma((4,)), dma((total,)), dma((total,))],
+        scratch_shapes=[held, held, pltpu.VMEM((rows, columns, LANES), jnp.float32), notes, notes, dma((8,)), dma((8,)), dma((total,)), dma((total,))],
         compiler_params=params(3),
     )(spread(arrived), wide, first, ratio, norm_next, square)
 

time: 144 us -> 134 us (0.931)
  Pallas kernels: 128 us -> 118 us
    pallas_call x1, Pallas kernels: 25.6 us -> 20.4 us  [body(): pl.pallas_call(system_kernel, out_shape=(shape(rows, columns, LANES), sha...]
    pallas_call x1, Pallas kernels: 23.1 us -> 20.7 us  [body(): pl.pallas_call(last_kernel, out_shape=(shape(levels, columns, latitudes),...]
    pallas_call x1, Pallas kernels: 31.7 us -> 29.3 us  [body(): pl.pallas_call(first_kernel, out_shape=(shape(slots, groups, LANES), shap...]
where the time goes in v5:
time: 134 us; the launch traced here: 133 us
  Pallas kernels  118 us (88%)
  local copies, waits for them, and re-layouts  9.44 us (7%)
  other arithmetic  4.85 us (4%)
  between operations  1.35 us (1%)
    pallas_call x1, Pallas kernels, body(): pl.pallas_call(return_kernel, out_shape=(shape(slots, groups, LANES), sha...  38.1 us
    pallas_call x1, Pallas kernels, body(): pl.pallas_call(first_kernel, out_shape=(shape(slots, groups, LANES), shap...  29.3 us
    pallas_call x1, Pallas kernels, body(): pl.pallas_call(last_kernel, out_shape=(shape(levels, columns, latitudes),...  20.7 us
    pallas_call x1, Pallas kernels, body(): pl.pallas_call(system_kernel, out_shape=(shape(rows, columns, LANES), sha...  20.4 us
    unnamed x16, local copies, waits for them, and re-layouts  7.96 us
    pallas_call x2, Pallas kernels, spread(): pl.pallas_call(spread_kernel, out_shape=shape(rows + 1, columns, LANES),...  6.12 us
    pallas_call x1, Pallas kernels, body(): pl.pallas_call(sample_kernel, out_shape=shape(slots, groups, LANES), in_s...  2.97 us

profile of v5, /device:TPU:0, one launch (start us, length us, event | category | flops | bytes accessed | tf_op | source)
XLA Modules:
  0.0 133.3 jit_solution(13841217718526192179)
XLA Ops:
  1.3 0.7 add_convert_fusion
  2.0 0.1 copy.15
  2.1 0.0 copy-start.2
  2.1 1.2 copy-done.2
  3.3 1.1 copy-done.3
  4.4 1.1 copy-done.4
  5.5 1.1 copy-done.5
  6.6 0.9 copy-done.6
  7.5 0.7 copy-done.7
  8.2 29.3 %shard_map.104 = (f32[256,4,128]{2,1,0:T(4,128)S(1)}, f32[32,128]{1,0:T(8,128)S(1)}, f32[512,512]{1,0:T(8,128)S(1)}, f32[128,512]{1,0:T(8,128)S(1)}, f32[256,128...) custom-call(s32[1]{0:T(128)S(6)} %copy.18.count, ...), custom_call_target="tpu_custom_call" | custom-call | tf_op jit(solution)/shard_map/pallas_call | solution.py:581
  37.5 0.1 copy.16
  37.6 0.1 copy.17
  37.7 0.1 convert_element_type.23.anchors
  37.8 3.1 %shard_map.105.field = f32[33,40,128]{2,1,0:T(8,128)S(1)} custom-call(s32[512]{0:T(512)S(1)} %convert_element_type.23.anchors, f32[256,4,128]{2,1,0:T(4,128)S(1)} %get-tuple-element.24.rows), custom_call_target="tpu_custom_call" | custom-call | tf_op jit(solution)/shard_map/pallas_call | solution.py:603
  40.9 1.9 %copy-done = f32[3,36,56,128]{3,2,1,0:T(8,128)S(1)} copy-done((f32[3,36,56,128]{3,2,1,0:T(8,128)S(1)}, f32[3,36,56,128]{3,2,1,0:T(8,128)}, u32[]{:S(2)}) %copy-start) | copy-done | bytes 3096600
  42.7 20.4 %shard_map.106 = (f32[32,40,128]{2,1,0:T(8,128)S(1)}, f32[32,40,128]{2,1,0:T(8,128)S(1)}, f32[33,40,128]{2,1,0:T(8,128)S(1)}, f32[8,128]{1,0:T(8,128)S(1)}) custom-call(f32[33,40,128]{2,1,0:T(8,128)S(1)} %shard_map.105.field, f32[3,36,56,128]{3,2,1,0:T(8,128)S(1)} %copy-done), custom_call_target="tpu_custom_call" | custom-call | tf_op jit(solution)/shard_map/pallas_call | solution.py:612
  63.2 3.0 %shard_map.107.rows = f32[256,4,128]{2,1,0:T(4,128)S(1)} custom-call(s32[512]{0:T(512)S(1)} %convert_element_type.23.anchors, f32[33,40,128]{2,1,0:T(8,128)S(1)} %get-tuple-element.26.field), custom_call_target="tpu_custom_call" | custom-call | tf_op jit(solution)/shard_map/pallas_call | solution.py:621
  66.2 38.1 %shard_map.108 = (f32[256,4,128]{2,1,0:T(4,128)S(1)}, f32[32,40,128]{2,1,0:T(8,128)S(1)}, f32[128,512]{1,0:T(8,128)S(1)}, f32[8,128]{1,0:T(8,128)S(1)}, f32[8,12...) custom-call(f32[256,4,128]{2,1,0:T(4,128)S(1)} %shard_map.107.rows, ...), custom_call_target="tpu_custom_call" | custom-call | tf_op jit(solution)/shard_map/pallas_call | solution.py:629
  104.2 0.5 slice.10
  104.8 3.1 %shard_map.109.field = f32[33,40,128]{2,1,0:T(8,128)S(1)} custom-call(s32[512]{0:T(512)S(1)} %convert_element_type.23.anchors, f32[256,4,128]{2,1,0:T(4,128)S(1)} %get-tuple-element.35.rows), custom_call_target="tpu_custom_call" | custom-call | tf_op jit(solution)/shard_map/pallas_call | solution.py:603
  107.8 20.7 %shard_map.110 = (f32[32,40,128]{2,1,0:T(8,128)S(1)}, f32[8,128]{1,0:T(8,128)S(1)}) custom-call(f32[33,40,128]{2,1,0:T(8,128)S(1)} %shard_map.109.field, f32[3,36,56,128]{3,2,1,0:T(8,128)S(1)} %copy-done.1, f32[32,40,128]{2,1,0:T(8,128)S(1)} %get-tuple-element.36.earlier, f32[8,128]{1,0:T(8,128)S(1)} %get-tuple-element.37.ratio, ...), custom_call_target="tpu_custom_call" | custom-call | tf_op jit(solution)/shard_map/pallas_call | solution.py:641
  128.6 0.6 slice.11
  129.2 2.2 %multiply_add_fusion = f32[32,40,128]{2,1,0:T(8,128)} fusion(f32[32,40,128]{2,1,0:T(8,128)S(1)} %get-tuple-element.43, f32[32,40,128]{2,1,0:T(8,128)S(1)} %get-tuple-element.42, f32[]{:T(128)} %bitcast.8, f32[]{:T(128)} %bitcast.7), kind=kLoop, calls=%fused_computation | loop fusion | flops 491520 | bytes 1966088 | tf_op jit(solution)/shard_map/add | solution.py:652
  131.3 2.0 %multiply_add_fusion.1 = f32[128,512]{1,0:T(8,128)} fusion(f32[128,512]{1,0:T(8,128)S(1)} %get-tuple-element.41, f32[128,512]{1,0:T(8,128)S(1)} %get-tuple-element.29.start, f32[]{:T(128)} %bitcast.8, f32[]{:T(128)} %bitcast.7), kind=kLoop, calls=%fused_computation.1 | loop fusion | flops 196608 | bytes 786440 | tf_op jit(solution)/shard_map/add | solution.py:651
  (11 shorter events, 0.0 us)
Async XLA Ops:
  2.1 1.2 copy-start.2
  3.3 1.1 copy-start.3
  4.4 1.1 copy-start.4
  5.5 1.1 copy-start.5
  6.6 0.9 copy-start.6
  7.5 0.7 copy-start.7
  40.9 1.9 %copy-start = (f32[3,36,56,128]{3,2,1,0:T(8,128)S(1)}, f32[3,36,56,128]{3,2,1,0:T(8,128)}, u32[]{:S(2)}) copy-start(f32[3,36,56,128]{3,2,1,0:T(8,128)} %get-tuple-element.25.wide_in.wide) | copy-start | bytes 9289732
  63.2 44.7 %copy-start.1 = (f32[3,36,56,128]{3,2,1,0:T(8,128)S(1)}, f32[3,36,56,128]{3,2,1,0:T(8,128)}, u32[]{:S(2)}) copy-start(f32[3,36,56,128]{3,2,1,0:T(8,128)} %get-tuple-element.25.wide_in.wide) | copy-start | bytes 9289732

commit v6 on v5

--- a/solution.py
+++ b/solution.py
@@ -550,11 +550,11 @@
     return jax.ShapeDtypeStruct(sizes, jnp.float32)
 
 
-def params(collective_id=None):
+def params(collective_id=None, limit=LIMIT):
     if collective_id is None:
         return pltpu.CompilerParams(vmem_limit_bytes=LIMIT)
     return pltpu.CompilerParams(
-        collective_id=collective_id, has_side_effects=True, vmem_limit_bytes=LIMIT
+        collective_id=collective_id, has_side_effects=True, vmem_limit_bytes=limit
     )
 
 
@@ -594,7 +594,7 @@
             pltpu.VMEM((3, levels, columns, latitudes), jnp.float32),
             *[dma((total,))] * 4, dma((8,)), dma((8,)), dma((4,)),
         ],
-        compiler_params=params(0),
+        compiler_params=params(0, 60 * 1024 * 1024),
     )(block_count, block_owner.reshape(1, block_total), spot, innovations, error_weight[0], courant_lon, courant_lat, background_std)
 
     corners = anchors[:, : 2 * DEPTH].reshape(total, 2, DEPTH).transpose(1, 0, 2).reshape(-1).astype(jnp.int32)

time: 134 us -> 132 us (0.985)
  local copies, waits for them, and re-layouts: 9.44 us -> 5.04 us
  Pallas kernels: 118 us -> 120 us
    unnamed x16, local copies, waits for them, and re-layouts: 7.96 us -> 2.94 us
    pallas_call x1, Pallas kernels: 29.3 us -> 31.2 us  [body(): pl.pallas_call(first_kernel, out_shape=(shape(slots, groups, LANES), shap...]
where the time goes in v6:
time: 132 us; the launch traced here: 131 us
  Pallas kernels  120 us (91%)
  other arithmetic  5.57 us (4%)
  local copies, waits for them, and re-layouts  5.04 us (4%)
  between operations  1.36 us (1%)
    pallas_call x1, Pallas kernels, body(): pl.pallas_call(return_kernel, out_shape=(shape(slots, groups, LANES), sha...  38.1 us
    pallas_call x1, Pallas kernels, body(): pl.pallas_call(first_kernel, out_shape=(shape(slots, groups, LANES), shap...  31.2 us
    pallas_call x1, Pallas kernels, body(): pl.pallas_call(last_kernel, out_shape=(shape(levels, columns, latitudes),...  21 us
    pallas_call x1, Pallas kernels, body(): pl.pallas_call(system_kernel, out_shape=(shape(rows, columns, LANES), sha...  20.2 us
    pallas_call x2, Pallas kernels, spread(): pl.pallas_call(spread_kernel, out_shape=shape(rows + 1, columns, LANES),...  6.01 us
    pallas_call x1, Pallas kernels, body(): pl.pallas_call(sample_kernel, out_shape=shape(slots, groups, LANES), in_s...  2.97 us
    unnamed x16, local copies, waits for them, and re-layouts  2.94 us

profile of v6, /device:TPU:0, one launch (start us, length us, event | category | flops | bytes accessed | tf_op | source)
XLA Modules:
  0.0 131.5 jit_solution(17733358401613711428)
XLA Ops:
  1.3 0.7 add_convert_fusion
  2.0 0.1 copy.15
  2.1 0.6 pad.4.spot
  2.7 31.2 %shard_map.104 = (f32[256,4,128]{2,1,0:T(4,128)}, f32[32,128]{1,0:T(8,128)}, f32[512,512]{1,0:T(8,128)}, f32[128,512]{1,0:T(8,128)}, f32[256,128]{1,0:T(8,128)},...) custom-call(s32[1]{0:T(128)S(6)} %copy.18.count, s32[1,128]{1,0:T(1,128)} %bitcast.13, ...), custom_call_target="tpu_custom_call" | custom-call | tf_op jit(solution)/shard_map/pallas_call | solution.py:581
  33.9 0.7 slice_convert_fusion
  34.6 0.1 copy.16
  34.7 0.1 copy.17
  34.8 0.1 convert_element_type.23.anchors
  34.9 0.0 copy-start.4
  34.9 1.0 copy-done.4
  35.9 3.0 %shard_map.105.field = f32[33,40,128]{2,1,0:T(8,128)S(1)} custom-call(s32[512]{0:T(512)S(1)} %convert_element_type.23.anchors, f32[256,4,128]{2,1,0:T(4,128)S(1)} %copy-done.4), custom_call_target="tpu_custom_call" | custom-call | tf_op jit(solution)/shard_map/pallas_call | solution.py:603
  38.9 1.9 %copy-done = f32[3,36,56,128]{3,2,1,0:T(8,128)S(1)} copy-done((f32[3,36,56,128]{3,2,1,0:T(8,128)S(1)}, f32[3,36,56,128]{3,2,1,0:T(8,128)}, u32[]{:S(2)}) %copy-start) | copy-done | bytes 3096600
  40.8 20.2 %shard_map.106 = (f32[32,40,128]{2,1,0:T(8,128)S(1)}, f32[32,40,128]{2,1,0:T(8,128)S(1)}, f32[33,40,128]{2,1,0:T(8,128)S(1)}, f32[8,128]{1,0:T(8,128)S(1)}) custom-call(f32[33,40,128]{2,1,0:T(8,128)S(1)} %shard_map.105.field, f32[3,36,56,128]{3,2,1,0:T(8,128)S(1)} %copy-done), custom_call_target="tpu_custom_call" | custom-call | tf_op jit(solution)/shard_map/pallas_call | solution.py:612
  61.0 0.0 copy-start.1
  61.1 3.0 %shard_map.107.rows = f32[256,4,128]{2,1,0:T(4,128)S(1)} custom-call(s32[512]{0:T(512)S(1)} %convert_element_type.23.anchors, f32[33,40,128]{2,1,0:T(8,128)S(1)} %get-tuple-element.26.field), custom_call_target="tpu_custom_call" | custom-call | tf_op jit(solution)/shard_map/pallas_call | solution.py:621
  64.0 0.0 copy-done.2
  64.0 0.0 copy-done.6
  64.1 38.1 %shard_map.108 = (f32[256,4,128]{2,1,0:T(4,128)S(1)}, f32[32,40,128]{2,1,0:T(8,128)S(1)}, f32[128,512]{1,0:T(8,128)S(1)}, f32[8,128]{1,0:T(8,128)S(1)}, f32[8,12...) custom-call(f32[256,4,128]{2,1,0:T(4,128)S(1)} %shard_map.107.rows, ...), custom_call_target="tpu_custom_call" | custom-call | tf_op jit(solution)/shard_map/pallas_call | solution.py:629
  102.2 0.5 slice.10
  102.7 3.0 %shard_map.109.field = f32[33,40,128]{2,1,0:T(8,128)S(1)} custom-call(s32[512]{0:T(512)S(1)} %convert_element_type.23.anchors, f32[256,4,128]{2,1,0:T(4,128)S(1)} %get-tuple-element.35.rows), custom_call_target="tpu_custom_call" | custom-call | tf_op jit(solution)/shard_map/pallas_call | solution.py:603
  105.7 21.0 %shard_map.110 = (f32[32,40,128]{2,1,0:T(8,128)S(1)}, f32[8,128]{1,0:T(8,128)S(1)}) custom-call(f32[33,40,128]{2,1,0:T(8,128)S(1)} %shard_map.109.field, f32[3,36,56,128]{3,2,1,0:T(8,128)S(1)} %copy-done.1, f32[32,40,128]{2,1,0:T(8,128)S(1)} %get-tuple-element.36.earlier, f32[8,128]{1,0:T(8,128)S(1)} %get-tuple-element.37.ratio, ...), custom_call_target="tpu_custom_call" | custom-call | tf_op jit(solution)/shard_map/pallas_call | solution.py:641
  126.7 0.6 slice.11
  127.3 2.2 %multiply_add_fusion = f32[32,40,128]{2,1,0:T(8,128)} fusion(f32[32,40,128]{2,1,0:T(8,128)S(1)} %get-tuple-element.43, f32[32,40,128]{2,1,0:T(8,128)S(1)} %get-tuple-element.42, f32[]{:T(128)} %bitcast.8, f32[]{:T(128)} %bitcast.7), kind=kLoop, calls=%fused_computation | loop fusion | flops 491520 | bytes 1966088 | tf_op jit(solution)/shard_map/add | solution.py:652
  129.5 2.0 %multiply_add_fusion.1 = f32[128,512]{1,0:T(8,128)} fusion(f32[128,512]{1,0:T(8,128)S(1)} %get-tuple-element.41, f32[128,512]{1,0:T(8,128)S(1)} %copy-done.3, f32[]{:T(128)} %bitcast.8, f32[]{:T(128)} %bitcast.7), kind=kLoop, calls=%fused_computation.1 | loop fusion | flops 196608 | bytes 786440 | tf_op jit(solution)/shard_map/add | solution.py:651
  (11 shorter events, 0.0 us)
Async XLA Ops:
  34.9 1.0 copy-start.4
  35.9 28.1 %copy-start.2 = (f32[512,512]{1,0:T(8,128)S(1)}, f32[512,512]{1,0:T(8,128)}, u32[]{:S(2)}) copy-start(f32[512,512]{1,0:T(8,128)} %get-tuple-element.28.matrix) | copy-start | bytes 3145732
  35.9 28.1 %copy-start.6 = (f32[256,128]{1,0:T(8,128)S(1)}, f32[256,128]{1,0:T(8,128)}, u32[]{:S(2)}) copy-start(f32[256,128]{1,0:T(8,128)} %get-tuple-element.30.packing) | copy-start | bytes 393220
  35.9 28.1 %copy-start.7 = (f32[8,128]{1,0:T(8,128)S(1)}, f32[8,128]{1,0:T(8,128)}, u32[]{:S(2)}) copy-start(f32[8,128]{1,0:T(8,128)} %get-tuple-element.32.norm) | copy-start | bytes 12292
  38.9 1.9 %copy-start = (f32[3,36,56,128]{3,2,1,0:T(8,128)S(1)}, f32[3,36,56,128]{3,2,1,0:T(8,128)}, u32[]{:S(2)}) copy-start(f32[3,36,56,128]{3,2,1,0:T(8,128)} %get-tuple-element.25.wide_in.wide) | copy-start | bytes 9289732
  40.8 23.3 %copy-start.3 = (f32[128,512]{1,0:T(8,128)S(1)}, f32[128,512]{1,0:T(8,128)}, u32[]{:S(2)}) copy-start(f32[128,512]{1,0:T(8,128)} %get-tuple-element.29.start) | copy-start | bytes 786436
  40.8 23.3 %copy-start.5 = (f32[32,8,512]{2,1,0:T(8,128)S(1)}, f32[32,8,512]{2,1,0:T(8,128)}, u32[]{:S(2)}) copy-start(f32[32,8,512]{2,1,0:T(8,128)} %get-tuple-element.31.packed) | copy-start | bytes 1572868
  61.0 44.7 %copy-start.1 = (f32[3,36,56,128]{3,2,1,0:T(8,128)S(1)}, f32[3,36,56,128]{3,2,1,0:T(8,128)}, u32[]{:S(2)}) copy-start(f32[3,36,56,128]{3,2,1,0:T(8,128)} %get-tuple-element.25.wide_in.wide) | copy-start | bytes 9289732
